TPU v7x, 512 devices: a whole 4x8x8 slice. The times are simulated.
512 devices in a mesh: blk: 256 (over y, x, z_hi, core), pr: 2 (over z_lo).
Axes of the slice: x: 4, y: 8, z: 8 (z_hi: 4, z_lo: 2; z = z_hi * 2 + z_lo), core: 2. Of those that a mesh axis runs over, the one named last changes fastest.
Arguments:
- coords: float32 [3, 524288], P(None, 'blk'), may hold values from -4 to 4
- probes: float32 [64, 524288], P('pr', 'blk'), may hold values from -6 to 6
- solves: float32 [64, 524288], P(None, 'blk'), may hold values from -6 to 6
- alpha: float32 [524288], P('blk'), may hold values from -6 to 6
- lengthscale: float32 [1], replicated, may hold values from 0.6 to 1.6
- column_pick: int32 [64], replicated, may hold values from 0 to 63, as said below
- plan: int32 [3, 256], replicated, may hold values from 0 to 255, as said below
Outputs:
- kernel_probes: float32 [64, 524288], P('pr', 'blk')
- slope_probes: float32 [64, 524288], P('pr', 'blk')
- gradients: float32 [2], replicated
Inputs may be any that keep to these rules, and one draw needn't show every extreme that they name: Row r of plan is block index xor s_r for a round value s_r of 1 to 255, distinct over rows; 256 is a power of two. `column_pick`: A permutation of 0 to 63.
All inputs are finite; a program needn't handle non-finite values.
Results may differ from a plain program's by a relative error of at most 0.00012.
Values sent between devices are 32-bit elements; how exact they have to be, the bound alone decides.
A program may use at most 128 MiB of HBM per device.

v0:
```python
import jax
import jax.numpy as jnp
from jax import lax
from jax.sharding import PartitionSpec as P

ROUNDS = 3


def from_partner(block, axis, stride):
    count = lax.axis_size(axis)
    route = []
    for low in range(count):
        high = low | 1 << stride
        if high != low and high < count:
            route += [(low, high), (high, low)]
    return lax.ppermute(block, axis, route)


def tile_terms(rows_x, cols_x, scale_len):
    dist_sq = jnp.zeros((rows_x.shape[1], cols_x.shape[1]), jnp.float32)
    for component in range(3):
        offset = rows_x[component][:, None] - cols_x[component][None, :]
        dist_sq = dist_sq + offset * offset
    scaled = jnp.sqrt(5.0 * dist_sq) / scale_len
    decay = jnp.exp(-scaled)
    kernel = (1.0 + scaled + scaled * scaled / 3.0) * decay
    slope = scaled * scaled / (3.0 * scale_len) * (1.0 + scaled) * decay
    return (kernel, slope)


def hdot(left, right):
    return jnp.dot(left, right, precision=lax.Precision.HIGHEST, preferred_element_type=jnp.float32)


def fetch(pieces, shift_value, bit_list):
    for bit_no in bit_list:
        flag = jnp.bitwise_and(jnp.right_shift(shift_value, bit_no), 1) == 1
        moved = from_partner(pieces, "blk", bit_no)
        pieces = tuple((jnp.where(flag, fresh, stale) for fresh, stale in zip(moved, pieces)))
    return pieces


def row_terms(rows_x, rows_alpha, mate_x, mate_probes, mate_alpha, scale_len):
    kernel, slope = tile_terms(mate_x, rows_x, scale_len)
    kz_part = hdot(mate_probes, kernel)
    dkz_part = hdot(mate_probes, slope)
    quad_part = jnp.sum(hdot(mate_alpha, slope) * rows_alpha)
    return (kz_part, dkz_part, quad_part)


def local(coords, probes, solves, alpha, lengthscale, column_pick, plan):
    scale_len = lengthscale[0]
    block_index = lax.axis_index("blk")
    half_index = lax.axis_index("pr")
    nbits = lax.axis_size("blk").bit_length() - 1
    pr_count = lax.axis_size("pr")
    block_rows = probes.shape[1]
    width = probes.shape[0]
    total_cols = solves.shape[0]
    picks = lax.dynamic_slice_in_dim(column_pick, half_index * width, width)
    onehot = (picks[:, None] == jnp.arange(total_cols, dtype=jnp.int32)[None, :]).astype(
        jnp.float32
    )
    picked = hdot(onehot, solves)
    bit_list = list(range(nbits))
    row_count = block_rows // 2
    row_starts = [0, row_count]
    quad_weight = 1.0 / pr_count
    kz_acc = jnp.zeros((probes.shape[0], row_count * len(row_starts)), jnp.float32)
    dkz_acc = jnp.zeros_like(kz_acc)
    quad_total = jnp.float32(0.0)
    for round_no in range(ROUNDS):
        entry = lax.dynamic_index_in_dim(plan[round_no], block_index, keepdims=False)
        shift_value = jnp.bitwise_xor(entry, block_index)
        mate_x, mate_probes, mate_alpha = fetch((coords, probes, alpha), shift_value, bit_list)
        kz_list = []
        dkz_list = []
        quad_round = jnp.float32(0.0)
        for start in row_starts:
            rows_x = lax.dynamic_slice_in_dim(coords, start, row_count, 1)
            rows_alpha = lax.dynamic_slice_in_dim(alpha, start, row_count, 0)
            kz_part, dkz_part, quad_part = row_terms(
                rows_x, rows_alpha, mate_x, mate_probes, mate_alpha, scale_len
            )
            kz_list.append(kz_part)
            dkz_list.append(dkz_part)
            quad_round = quad_round + quad_part
        kz_acc = kz_acc + jnp.concatenate(kz_list, axis=1)
        dkz_acc = dkz_acc + jnp.concatenate(dkz_list, axis=1)
        quad_total = quad_total + lax.psum(quad_round * quad_weight, ("blk", "pr"))
    kernel_probes, slope_probes = (kz_acc, dkz_acc)
    noise_local = jnp.sum(alpha * alpha) / pr_count - jnp.sum(picked * probes) / total_cols
    trace_local = jnp.sum(picked * slope_probes) / total_cols
    noise_sum, trace_sum = lax.psum((noise_local, trace_local), ("blk", "pr"))
    slope_sum = quad_total - trace_sum
    gradients = jnp.stack([0.5 * noise_sum / block_rows, 0.5 * slope_sum / block_rows])
    return (kernel_probes, slope_probes, gradients)


def solution(mesh):
    placed = (P(None, "blk"), P("pr", "blk"), P(None, "blk"), P("blk"), P(), P(), P())
    return jax.shard_map(
        local,
        mesh=mesh,
        in_specs=placed,
        out_specs=(P("pr", "blk"), P("pr", "blk"), P()),
        check_vma=False,
    )
```

profile of v0, /device:TPU:1, one launch (start us, length us, event | category | flops | bytes accessed | tf_op | source)
XLA Modules:
  0.0 704.9 jit_solution(14171554963835879361)
XLA Ops:
  0.6 8.9 %collective-permute-start.44 = (f32[2048]{0:T(1024)}, f32[2048]{0:T(1024)S(1)}, u32[]{:S(2)}, u32[]{:S(2)}) collective-permute-start(f32[2048]{0:T(1024)} %param.10), channel_id=1, source_target_pairs={{0,2},{2,0},{4,6},{6,4},{8,10},{10,8},{12,14},{14,12},{16,18},{18,... | collective-permute-start | bytes 24584 | tf_op jit(solution)/shard_map/ppermute | solution.py:16
  23.9 4.2 collective-permute-start.52
  30.8 7.4 %collective-permute-start.46 = (f32[2048]{0:T(1024)S(1)}, f32[2048]{0:T(1024)S(1)}, u32[]{:S(2)}, u32[]{:S(2)}) collective-permute-start(f32[2048]{0:T(1024)S(1)} %broadcast_select_fusion.65), channel_id=1, source_target_pairs={{0,8},{8,0},{2,10},{10,2},{4,12},{12,4},{6,14},{14,6},{16,24},{24,... | collective-permute-start | bytes 24584 | tf_op jit(solution)/shard_map/ppermute | solution.py:16
  40.1 7.3 %collective-permute-start.60 = (f32[2048]{0:T(1024)S(1)}, f32[2048]{0:T(1024)S(1)}, u32[]{:S(2)}, u32[]{:S(2)}) collective-permute-start(f32[2048]{0:T(1024)S(1)} %broadcast_select_fusion.49), channel_id=1, source_target_pairs={{0,8},{8,0},{2,10},{10,2},{4,12},{12,4},{6,14},{14,6},{16,24},{24,... | collective-permute-start | bytes 24584 | tf_op jit(solution)/shard_map/ppermute | solution.py:16
  47.4 3.1 collective-permute-start.47
  58.8 4.0 collective-permute-start.23
  65.1 4.4 collective-permute-start.48
  71.0 4.3 collective-permute-start.55
  76.9 4.3 collective-permute-start.62
  82.8 3.2 collective-permute-start.49
  88.1 3.2 collective-permute-start.63
  91.3 4.2 collective-permute-start.50
  100.5 6.3 collective-permute-start.24
  106.8 4.2 collective-permute-start.64
  114.0 4.8 collective-permute-start.51
  118.8 3.5 collective-permute-done.51
  122.3 4.7 collective-permute-start.58
  127.1 3.5 collective-permute-done.58
  130.6 4.7 collective-permute-start.65
  135.4 3.5 collective-permute-done.65
  146.5 4.7 collective-permute-start.12
  153.4 4.7 collective-permute-start.40
  160.2 3.2 collective-permute-start.27
  167.9 3.9 collective-permute-start.28
  174.1 7.1 %collective-permute-start.15 = (f32[3,2048]{1,0:T(4,128)S(1)}, f32[3,2048]{1,0:T(4,128)S(1)}, u32[]{:S(2)}, u32[]{:S(2)}) collective-permute-start(f32[3,2048]{1,0:T(4,128)S(1)} %broadcast_select_fusion.46), channel_id=1, source_target_pairs={{0,256},{256,0},{2,258},{258,2},{4,260},{260,4},{6,262},{262,6},{8... | collective-permute-start | bytes 73736 | tf_op jit(solution)/shard_map/ppermute | solution.py:16
  183.4 7.3 %collective-permute-start.43 = (f32[3,2048]{1,0:T(4,128)S(1)}, f32[3,2048]{1,0:T(4,128)S(1)}, u32[]{:S(2)}, u32[]{:S(2)}) collective-permute-start(f32[3,2048]{1,0:T(4,128)S(1)} %broadcast_select_fusion.30), channel_id=1, source_target_pairs={{0,256},{256,0},{2,258},{258,2},{4,260},{260,4},{6,262},{262,6},{8... | collective-permute-start | bytes 73736 | tf_op jit(solution)/shard_map/ppermute | solution.py:16
  192.1 12.2 %fusion.56 = f32[1,1024]{1,0:T(1,128)S(1)} fusion(f32[2048,1]{0,1:T(1,128)S(1)} %bitcast.73, f32[]{:T(128)S(6)} %mul.235, f32[]{:T(128)} %bitcast.69, f32[1024]{0:T(1024)S(1)} %bitcast.167, f32[2048]{0:T(1024)S(1)} %bitcast.83, f32[1024]{0:T(1024)S(1)} %bitcast.176, f32[2048]{0:T(1024)S(1)} %bitcast.89, f32[1024]{0:T(1024)S(1)} %bitcast.158, ...), kind=kOutput, calls=%fused_computation.74 | convolution fusion | flops 58720256 | bytes 49160 | tf_op jit(solution)/shard_map/dot_general | solution.py:32
  204.3 12.4 %fusion.58 = f32[1,1024]{1,0:T(1,128)S(1)} fusion(f32[2048,1]{0,1:T(1,128)S(1)} %bitcast.74, f32[]{:T(128)S(6)} %mul.235, f32[]{:T(128)} %bitcast.70, f32[1024]{0:T(1024)S(1)} %bitcast.131, f32[2048]{0:T(1024)S(1)} %bitcast.84, f32[1024]{0:T(1024)S(1)} %bitcast.140, f32[2048]{0:T(1024)S(1)} %bitcast.90, f32[1024]{0:T(1024)S(1)} %bitcast.149, ...), kind=kOutput, calls=%fused_computation.76 | convolution fusion | flops 58720256 | bytes 49160 | tf_op jit(solution)/shard_map/dot_general | solution.py:32
  216.8 12.2 %fusion.48 = f32[1,1024]{1,0:T(1,128)S(1)} fusion(f32[2048,1]{0,1:T(1,128)S(1)} %bitcast.75, f32[]{:T(128)S(6)} %mul.235, f32[]{:T(128)} %bitcast.61, f32[1024]{0:T(1024)S(1)} %bitcast.132, f32[2048]{0:T(1024)S(1)} %bitcast.101, f32[1024]{0:T(1024)S(1)} %bitcast.141, f32[2048]{0:T(1024)S(1)} %bitcast.107, f32[1024]{0:T(1024)S(1)} %bitcast.150, ...), kind=kOutput, calls=%fused_computation.66 | convolution fusion | flops 58720256 | bytes 49160 | tf_op jit(solution)/shard_map/dot_general | solution.py:32
  229.0 12.4 %fusion.52 = f32[1,1024]{1,0:T(1,128)S(1)} fusion(f32[2048,1]{0,1:T(1,128)S(1)} %bitcast.76, f32[]{:T(128)S(6)} %mul.235, f32[]{:T(128)} %bitcast.65, f32[1024]{0:T(1024)S(1)} %bitcast.168, f32[2048]{0:T(1024)S(1)} %bitcast.102, f32[1024]{0:T(1024)S(1)} %bitcast.177, f32[2048]{0:T(1024)S(1)} %bitcast.108, f32[1024]{0:T(1024)S(1)} %bitcast.159, ...), kind=kOutput, calls=%fused_computation.70 | convolution fusion | flops 58720256 | bytes 49160 | tf_op jit(solution)/shard_map/dot_general | solution.py:32
  241.4 12.2 %fusion.54 = f32[1,1024]{1,0:T(1,128)S(1)} fusion(f32[2048,1]{0,1:T(1,128)S(1)} %bitcast.71, f32[]{:T(128)S(6)} %mul.235, f32[]{:T(128)} %bitcast.66, f32[1024]{0:T(1024)S(1)} %bitcast.169, f32[2048]{0:T(1024)S(1)} %bitcast.119, f32[1024]{0:T(1024)S(1)} %bitcast.178, f32[2048]{0:T(1024)S(1)} %bitcast.125, f32[1024]{0:T(1024)S(1)} %bitcast.160, ...), kind=kOutput, calls=%fused_computation.72 | convolution fusion | flops 58720256 | bytes 49160 | tf_op jit(solution)/shard_map/dot_general | solution.py:32
  253.7 4.0 collective-permute-start.1
  257.7 12.4 %fusion.50 = f32[1,1024]{1,0:T(1,128)S(1)} fusion(f32[2048,1]{0,1:T(1,128)S(1)} %bitcast.72, f32[]{:T(128)S(6)} %mul.235, f32[]{:T(128)} %bitcast.62, f32[1024]{0:T(1024)S(1)} %bitcast.133, f32[2048]{0:T(1024)S(1)} %bitcast.120, f32[1024]{0:T(1024)S(1)} %bitcast.142, f32[2048]{0:T(1024)S(1)} %bitcast.126, f32[1024]{0:T(1024)S(1)} %bitcast.151, ...), kind=kOutput, calls=%fused_computation.68 | convolution fusion | flops 58720256 | bytes 49160 | tf_op jit(solution)/shard_map/dot_general | solution.py:32
  276.7 4.0 collective-permute-start.30
  280.8 6.1 collective-permute-start.2
  286.9 8.1 %collective-permute-done.16 = f32[32,2048]{1,0:T(8,128)S(1)} collective-permute-done((f32[32,2048]{1,0:T(8,128)S(1)}, f32[32,2048]{1,0:T(8,128)S(1)}, u32[]{:S(2)}, u32[]{:S(2)}) %collective-permute-start.16) | collective-permute-done | bytes 262176 | tf_op jit(solution)/shard_map/ppermute | solution.py:16
  295.0 5.3 collective-permute-start.17
  300.4 3.8 collective-permute-start.31
  307.4 9.1 %collective-permute-done.17 = f32[32,2048]{1,0:T(8,128)S(1)} collective-permute-done((f32[32,2048]{1,0:T(8,128)S(1)}, f32[32,2048]{1,0:T(8,128)S(1)}, u32[]{:S(2)}, u32[]{:S(2)}) %collective-permute-start.17) | collective-permute-done | bytes 262176 | tf_op jit(solution)/shard_map/ppermute | solution.py:16
  316.6 3.7 collective-permute-start.18
  322.6 3.6 collective-permute-start.32
  328.5 4.5 collective-permute-start.19
  337.5 3.4 collective-permute-start.5
  343.1 3.4 collective-permute-start.20
  348.8 3.4 collective-permute-start.34
  352.2 4.8 collective-permute-start.6
  359.0 4.3 collective-permute-start.35
  363.4 8.3 %collective-permute-start.7 = (f32[32,2048]{1,0:T(8,128)S(1)}, f32[32,2048]{1,0:T(8,128)S(1)}, u32[]{:S(2)}, u32[]{:S(2)}) collective-permute-start(f32[32,2048]{1,0:T(8,128)S(1)} %broadcast_select_fusion.22), channel_id=1, source_target_pairs={{0,256},{256,0},{2,258},{258,2},{4,260},{260,4},{6,262},{262,6},{8... | collective-permute-start | bytes 786440 | tf_op jit(solution)/shard_map/ppermute | solution.py:16
  371.7 7.3 %collective-permute-start.22 = (f32[32,2048]{1,0:T(8,128)S(1)}, f32[32,2048]{1,0:T(8,128)S(1)}, u32[]{:S(2)}, u32[]{:S(2)}) collective-permute-start(f32[32,2048]{1,0:T(8,128)S(1)} %broadcast_select_fusion.14), channel_id=1, source_target_pairs={{0,256},{256,0},{2,258},{258,2},{4,260},{260,4},{6,262},{262,6},{8... | collective-permute-start | bytes 786440 | tf_op jit(solution)/shard_map/ppermute | solution.py:16
  379.0 18.5 %collective-permute-done.35 = f32[32,2048]{1,0:T(8,128)S(1)} collective-permute-done((f32[32,2048]{1,0:T(8,128)S(1)}, f32[32,2048]{1,0:T(8,128)S(1)}, u32[]{:S(2)}, u32[]{:S(2)}) %collective-permute-start.35) | collective-permute-done | bytes 262176 | tf_op jit(solution)/shard_map/ppermute | solution.py:16
  397.6 7.1 %collective-permute-start.36 = (f32[32,2048]{1,0:T(8,128)S(1)}, f32[32,2048]{1,0:T(8,128)S(1)}, u32[]{:S(2)}, u32[]{:S(2)}) collective-permute-start(f32[32,2048]{1,0:T(8,128)S(1)} %broadcast_select_fusion.6), channel_id=1, source_target_pairs={{0,256},{256,0},{2,258},{258,2},{4,260},{260,4},{6,262},{262,6},{8... | collective-permute-start | bytes 786440 | tf_op jit(solution)/shard_map/ppermute | solution.py:16
  404.7 12.9 %fusion.57 = f32[32,1024]{1,0:T(8,128)S(1)} fusion(f32[32,2048]{1,0:T(8,128)S(1)} %broadcast_select_fusion.23, f32[]{:T(128)S(6)} %mul.235, f32[]{:T(128)} %bitcast.52, f32[1024]{0:T(1024)S(1)} %bitcast.170, f32[2048]{0:T(1024)S(1)} %bitcast.85, f32[1024]{0:T(1024)S(1)} %bitcast.179, f32[2048]{0:T(1024)S(1)} %bitcast.91, f32[1024]{0:T(1024)S(1)} %bitcast.161, ...), kind=kOutput, calls=%fused_computation.75 | convolution fusion | flops 838860800 | bytes 430088 | tf_op jit(solution)/shard_map/dot_general | solution.py:32
  417.7 12.9 %fusion.59 = f32[32,1024]{1,0:T(8,128)S(1)} fusion(f32[32,2048]{1,0:T(8,128)S(1)} %broadcast_select_fusion.23, f32[]{:T(128)S(6)} %mul.235, f32[]{:T(128)} %bitcast.58, f32[1024]{0:T(1024)S(1)} %bitcast.134, f32[2048]{0:T(1024)S(1)} %bitcast.86, f32[1024]{0:T(1024)S(1)} %bitcast.143, f32[2048]{0:T(1024)S(1)} %bitcast.92, f32[1024]{0:T(1024)S(1)} %bitcast.152, ...), kind=kOutput, calls=%fused_computation.77 | convolution fusion | flops 838860800 | bytes 430088 | tf_op jit(solution)/shard_map/dot_general | solution.py:32
  430.7 13.1 %fusion.53 = f32[32,1024]{1,0:T(8,128)S(1)} fusion(f32[32,2048]{1,0:T(8,128)S(1)} %broadcast_select_fusion.15, f32[]{:T(128)S(6)} %mul.235, f32[]{:T(128)} %bitcast.57, f32[1024]{0:T(1024)S(1)} %bitcast.171, f32[2048]{0:T(1024)S(1)} %bitcast.103, f32[1024]{0:T(1024)S(1)} %bitcast.180, f32[2048]{0:T(1024)S(1)} %bitcast.109, f32[1024]{0:T(1024)S(1)} %bitcast.162, ...), kind=kOutput, calls=%fused_computation.71 | convolution fusion | flops 838860800 | bytes 430088 | tf_op jit(solution)/shard_map/dot_general | solution.py:32
  443.8 12.9 %fusion.49 = f32[32,1024]{1,0:T(8,128)S(1)} fusion(f32[32,2048]{1,0:T(8,128)S(1)} %broadcast_select_fusion.15, f32[]{:T(128)S(6)} %mul.235, f32[]{:T(128)} %bitcast.56, f32[1024]{0:T(1024)S(1)} %bitcast.135, f32[2048]{0:T(1024)S(1)} %bitcast.104, f32[1024]{0:T(1024)S(1)} %bitcast.144, f32[2048]{0:T(1024)S(1)} %bitcast.110, f32[1024]{0:T(1024)S(1)} %bitcast.153, ...), kind=kOutput, calls=%fused_computation.67 | convolution fusion | flops 838860800 | bytes 430088 | tf_op jit(solution)/shard_map/dot_general | solution.py:32
  456.8 13.1 %fusion.55 = f32[32,1024]{1,0:T(8,128)S(1)} fusion(f32[32,2048]{1,0:T(8,128)S(1)} %broadcast_select_fusion.7, f32[]{:T(128)S(6)} %mul.235, f32[]{:T(128)} %bitcast.55, f32[1024]{0:T(1024)S(1)} %bitcast.172, f32[2048]{0:T(1024)S(1)} %bitcast.121, f32[1024]{0:T(1024)S(1)} %bitcast.181, f32[2048]{0:T(1024)S(1)} %bitcast.127, f32[1024]{0:T(1024)S(1)} %bitcast.163, ...), kind=kOutput, calls=%fused_computation.73 | convolution fusion | flops 838860800 | bytes 430088 | tf_op jit(solution)/shard_map/dot_general | solution.py:32
  470.0 12.9 %fusion.51 = f32[32,1024]{1,0:T(8,128)S(1)} fusion(f32[32,2048]{1,0:T(8,128)S(1)} %broadcast_select_fusion.7, f32[]{:T(128)S(6)} %mul.235, f32[]{:T(128)} %bitcast.54, f32[1024]{0:T(1024)S(1)} %bitcast.136, f32[2048]{0:T(1024)S(1)} %bitcast.122, f32[1024]{0:T(1024)S(1)} %bitcast.145, f32[2048]{0:T(1024)S(1)} %bitcast.128, f32[1024]{0:T(1024)S(1)} %bitcast.154, ...), kind=kOutput, calls=%fused_computation.69 | convolution fusion | flops 838860800 | bytes 430088 | tf_op jit(solution)/shard_map/dot_general | solution.py:32
  485.7 138.0 %all-reduce = (f32[]{:T(128)}, f32[]{:T(128)}, f32[]{:T(128)}) all-reduce(f32[]{:T(128)S(6)} %multiply.16, f32[]{:T(128)S(6)} %div.108, f32[]{:T(128)S(6)} %sub.276), channel_id=1, replica_groups=mesh['blk'=256,'pr'=2] {'blk','pr'}, use_global_device_ids=true, to_apply=%region_5.6 | all-reduce | flops 3 | bytes 24 | tf_op jit(solution)/shard_map/psum | solution.py:90
  625.6 13.1 %fusion.4 = f32[32,1024]{1,0:T(8,128)S(1)} fusion(f32[32,2048]{1,0:T(8,128)S(1)} %broadcast_select_fusion.7, f32[2048]{0:T(1024)S(1)} %bitcast.123, f32[2048]{0:T(1024)S(1)} %bitcast.129, f32[2048]{0:T(1024)S(1)} %bitcast.117, f32[]{:T(128)} %bitcast.64, f32[1024]{0:T(1024)S(1)} %bitcast.173, f32[1024]{0:T(1024)S(1)} %bitcast.182, f32[1024]{0:T(1024)S(1)} %bitcast.164), kind=kOutput, calls=%fused_computation.12 | convolution fusion | flops 838860800 | bytes 430084 | tf_op jit(solution)/shard_map/dot_general | solution.py:32
  638.7 12.9 %fusion = f32[32,1024]{1,0:T(8,128)S(1)} fusion(f32[32,2048]{1,0:T(8,128)S(1)} %broadcast_select_fusion.7, f32[2048]{0:T(1024)S(1)} %bitcast.124, f32[2048]{0:T(1024)S(1)} %bitcast.130, f32[2048]{0:T(1024)S(1)} %bitcast.118, f32[1024]{0:T(1024)S(1)} %bitcast.137, f32[1024]{0:T(1024)S(1)} %bitcast.146, f32[1024]{0:T(1024)S(1)} %bitcast.155, f32[]{:T(128)} %bitcast.60), kind=kOutput, calls=%fused_computation.6 | convolution fusion | flops 838860800 | bytes 430084 | tf_op jit(solution)/shard_map/dot_general | solution.py:32
  651.5 12.9 %fusion.12 = f32[32,1024]{1,0:T(8,128)S(1)} fusion(f32[32,2048]{1,0:T(8,128)S(1)} %broadcast_select_fusion.15, f32[2048]{0:T(1024)S(1)} %bitcast.105, f32[2048]{0:T(1024)S(1)} %bitcast.111, f32[2048]{0:T(1024)S(1)} %bitcast.99, f32[]{:T(128)} %bitcast.63, f32[1024]{0:T(1024)S(1)} %bitcast.174, f32[1024]{0:T(1024)S(1)} %bitcast.183, f32[1024]{0:T(1024)S(1)} %bitcast.165), kind=kOutput, calls=%fused_computation.24 | convolution fusion | flops 838860800 | bytes 430084 | tf_op jit(solution)/shard_map/dot_general | solution.py:32
  664.5 13.2 %fusion.8 = f32[32,1024]{1,0:T(8,128)S(1)} fusion(f32[32,2048]{1,0:T(8,128)S(1)} %broadcast_select_fusion.15, f32[2048]{0:T(1024)S(1)} %bitcast.106, f32[2048]{0:T(1024)S(1)} %bitcast.112, f32[2048]{0:T(1024)S(1)} %bitcast.100, f32[1024]{0:T(1024)S(1)} %bitcast.138, f32[1024]{0:T(1024)S(1)} %bitcast.147, f32[1024]{0:T(1024)S(1)} %bitcast.156, f32[]{:T(128)} %bitcast.59), kind=kOutput, calls=%fused_computation.18 | convolution fusion | flops 838860800 | bytes 430084 | tf_op jit(solution)/shard_map/dot_general | solution.py:32
  677.7 12.9 %fusion.20 = f32[32,1024]{1,0:T(8,128)S(1)} fusion(f32[32,2048]{1,0:T(8,128)S(1)} %copy-done.4, f32[]{:T(128)} %bitcast.67, f32[1024]{0:T(1024)S(1)} %bitcast.175, f32[2048]{0:T(1024)S(1)} %bitcast.87, f32[1024]{0:T(1024)S(1)} %bitcast.184, f32[2048]{0:T(1024)S(1)} %bitcast.93, f32[1024]{0:T(1024)S(1)} %bitcast.166, f32[2048]{0:T(1024)S(1)} %bitcast.81), kind=kOutput, calls=%fused_computation.36 | convolution fusion | flops 838860800 | bytes 430084 | tf_op jit(solution)/shard_map/dot_general | solution.py:32
  690.6 12.8 %fusion.16 = f32[32,1024]{1,0:T(8,128)S(1)} fusion(f32[32,2048]{1,0:T(8,128)S(1)} %copy-done.4, f32[1024]{0:T(1024)S(1)} %bitcast.139, f32[1024]{0:T(1024)S(1)} %bitcast.148, f32[1024]{0:T(1024)S(1)} %bitcast.157, f32[]{:T(128)} %bitcast.68, f32[2048]{0:T(1024)S(1)} %bitcast.88, f32[2048]{0:T(1024)S(1)} %bitcast.94, f32[2048]{0:T(1024)S(1)} %bitcast.82), kind=kOutput, calls=%fused_computation.30 | convolution fusion | flops 838860800 | bytes 430084 | tf_op jit(solution)/shard_map/dot_general | solution.py:32
  (191 shorter events, 87.4 us)
Async XLA Ops:
  0.6 17.2 %collective-permute-start.44 = (f32[2048]{0:T(1024)}, f32[2048]{0:T(1024)S(1)}, u32[]{:S(2)}, u32[]{:S(2)}) collective-permute-start(f32[2048]{0:T(1024)} %param.10), channel_id=1, source_target_pairs={{0,2},{2,0},{4,6},{6,4},{8,10},{10,8},{12,14},{14,12},{16,18},{18,... | collective-permute-start | bytes 24584 | tf_op jit(solution)/shard_map/ppermute | solution.py:16
  9.6 46.3 %collective-permute-start.8 = (f32[3,2048]{1,0:T(4,128)}, f32[3,2048]{1,0:T(4,128)S(1)}, u32[]{:S(2)}, u32[]{:S(2)}) collective-permute-start(f32[3,2048]{1,0:T(4,128)} %param.7), channel_id=1, source_target_pairs={{0,2},{2,0},{4,6},{6,4},{8,10},{10,8},{12,14},{14,12},{16,18},{18,... | collective-permute-start | bytes 73736 | tf_op jit(solution)/shard_map/ppermute | solution.py:16
  11.5 242.1 %collective-permute-start = (f32[32,2048]{1,0:T(8,128)}, f32[32,2048]{1,0:T(8,128)S(1)}, u32[]{:S(2)}, u32[]{:S(2)}) collective-permute-start(f32[32,2048]{1,0:T(8,128)} %param.8), channel_id=1, source_target_pairs={{0,2},{2,0},{4,6},{6,4},{8,10},{10,8},{12,14},{14,12},{16,18},{18,... | collective-permute-start | bytes 786440 | tf_op jit(solution)/shard_map/ppermute | solution.py:16
  19.2 11.6 %collective-permute-start.45 = (f32[2048]{0:T(1024)S(1)}, f32[2048]{0:T(1024)S(1)}, u32[]{:S(2)}, u32[]{:S(2)}) collective-permute-start(f32[2048]{0:T(1024)S(1)} %get-tuple-element.36), channel_id=1, source_target_pairs={{0,4},{4,0},{2,6},{6,2},{8,12},{12,8},{10,14},{14,10},{16,20},{20,... | collective-permute-start | bytes 24584 | tf_op jit(solution)/shard_map/ppermute | solution.py:16
  23.9 14.2 %collective-permute-start.52 = (f32[2048]{0:T(1024)S(1)}, f32[2048]{0:T(1024)S(1)}, u32[]{:S(2)}, u32[]{:S(2)}) collective-permute-start(f32[2048]{0:T(1024)S(1)} %get-tuple-element.38), channel_id=1, source_target_pairs={{0,4},{4,0},{2,6},{6,2},{8,12},{12,8},{10,14},{14,10},{16,20},{20,... | collective-permute-start | bytes 24584 | tf_op jit(solution)/shard_map/ppermute | solution.py:16
  28.2 11.9 %collective-permute-start.59 = (f32[2048]{0:T(1024)S(1)}, f32[2048]{0:T(1024)S(1)}, u32[]{:S(2)}, u32[]{:S(2)}) collective-permute-start(f32[2048]{0:T(1024)S(1)} %get-tuple-element.37), channel_id=1, source_target_pairs={{0,4},{4,0},{2,6},{6,2},{8,12},{12,8},{10,14},{14,10},{16,20},{20,... | collective-permute-start | bytes 24584 | tf_op jit(solution)/shard_map/ppermute | solution.py:16
  30.8 16.6 %collective-permute-start.46 = (f32[2048]{0:T(1024)S(1)}, f32[2048]{0:T(1024)S(1)}, u32[]{:S(2)}, u32[]{:S(2)}) collective-permute-start(f32[2048]{0:T(1024)S(1)} %broadcast_select_fusion.65), channel_id=1, source_target_pairs={{0,8},{8,0},{2,10},{10,2},{4,12},{12,4},{6,14},{14,6},{16,24},{24,... | collective-permute-start | bytes 24584 | tf_op jit(solution)/shard_map/ppermute | solution.py:16
  38.1 12.4 %collective-permute-start.53 = (f32[2048]{0:T(1024)S(1)}, f32[2048]{0:T(1024)S(1)}, u32[]{:S(2)}, u32[]{:S(2)}) collective-permute-start(f32[2048]{0:T(1024)S(1)} %broadcast_select_fusion.57), channel_id=1, source_target_pairs={{0,8},{8,0},{2,10},{10,2},{4,12},{12,4},{6,14},{14,6},{16,24},{24,... | collective-permute-start | bytes 24584 | tf_op jit(solution)/shard_map/ppermute | solution.py:16
  40.1 12.6 %collective-permute-start.60 = (f32[2048]{0:T(1024)S(1)}, f32[2048]{0:T(1024)S(1)}, u32[]{:S(2)}, u32[]{:S(2)}) collective-permute-start(f32[2048]{0:T(1024)S(1)} %broadcast_select_fusion.49), channel_id=1, source_target_pairs={{0,8},{8,0},{2,10},{10,2},{4,12},{12,4},{6,14},{14,6},{16,24},{24,... | collective-permute-start | bytes 24584 | tf_op jit(solution)/shard_map/ppermute | solution.py:16
  47.4 11.4 %collective-permute-start.47 = (f32[2048]{0:T(1024)S(1)}, f32[2048]{0:T(1024)S(1)}, u32[]{:S(2)}, u32[]{:S(2)}) collective-permute-start(f32[2048]{0:T(1024)S(1)} %broadcast_select_fusion.66), channel_id=1, source_target_pairs={{0,16},{16,0},{2,18},{18,2},{4,20},{20,4},{6,22},{22,6},{8,24},{24... | collective-permute-start | bytes 24584 | tf_op jit(solution)/shard_map/ppermute | solution.py:16
  50.5 12.3 %collective-permute-start.54 = (f32[2048]{0:T(1024)S(1)}, f32[2048]{0:T(1024)S(1)}, u32[]{:S(2)}, u32[]{:S(2)}) collective-permute-start(f32[2048]{0:T(1024)S(1)} %broadcast_select_fusion.58), channel_id=1, source_target_pairs={{0,16},{16,0},{2,18},{18,2},{4,20},{20,4},{6,22},{22,6},{8,24},{24... | collective-permute-start | bytes 24584 | tf_op jit(solution)/shard_map/ppermute | solution.py:16
  52.7 12.3 %collective-permute-start.61 = (f32[2048]{0:T(1024)S(1)}, f32[2048]{0:T(1024)S(1)}, u32[]{:S(2)}, u32[]{:S(2)}) collective-permute-start(f32[2048]{0:T(1024)S(1)} %broadcast_select_fusion.50), channel_id=1, source_target_pairs={{0,16},{16,0},{2,18},{18,2},{4,20},{20,4},{6,22},{22,6},{8,24},{24... | collective-permute-start | bytes 24584 | tf_op jit(solution)/shard_map/ppermute | solution.py:16
  56.7 29.3 %collective-permute-start.9 = (f32[3,2048]{1,0:T(4,128)S(1)}, f32[3,2048]{1,0:T(4,128)S(1)}, u32[]{:S(2)}, u32[]{:S(2)}) collective-permute-start(f32[3,2048]{1,0:T(4,128)S(1)} %get-tuple-element.20), channel_id=1, source_target_pairs={{0,4},{4,0},{2,6},{6,2},{8,12},{12,8},{10,14},{14,10},{16,20},{20,... | collective-permute-start | bytes 73736 | tf_op jit(solution)/shard_map/ppermute | solution.py:16
  58.8 32.5 %collective-permute-start.23 = (f32[3,2048]{1,0:T(4,128)S(1)}, f32[3,2048]{1,0:T(4,128)S(1)}, u32[]{:S(2)}, u32[]{:S(2)}) collective-permute-start(f32[3,2048]{1,0:T(4,128)S(1)} %get-tuple-element.19), channel_id=1, source_target_pairs={{0,4},{4,0},{2,6},{6,2},{8,12},{12,8},{10,14},{14,10},{16,20},{20,... | collective-permute-start | bytes 73736 | tf_op jit(solution)/shard_map/ppermute | solution.py:16
  62.9 35.7 %collective-permute-start.37 = (f32[3,2048]{1,0:T(4,128)S(1)}, f32[3,2048]{1,0:T(4,128)S(1)}, u32[]{:S(2)}, u32[]{:S(2)}) collective-permute-start(f32[3,2048]{1,0:T(4,128)S(1)} %get-tuple-element.18), channel_id=1, source_target_pairs={{0,4},{4,0},{2,6},{6,2},{8,12},{12,8},{10,14},{14,10},{16,20},{20,... | collective-permute-start | bytes 73736 | tf_op jit(solution)/shard_map/ppermute | solution.py:16
  65.1 5.9 collective-permute-start.48
  76.9 5.9 collective-permute-start.62
  86.0 9.6 %collective-permute-start.56 = (f32[2048]{0:T(1024)S(1)}, f32[2048]{0:T(1024)S(1)}, u32[]{:S(2)}, u32[]{:S(2)}) collective-permute-start(f32[2048]{0:T(1024)S(1)} %broadcast_select_fusion.60), channel_id=1, source_target_pairs={{0,64},{64,0},{2,66},{66,2},{4,68},{68,4},{6,70},{70,6},{8,72},{72... | collective-permute-start | bytes 24584 | tf_op jit(solution)/shard_map/ppermute | solution.py:16
  88.1 12.4 %collective-permute-start.63 = (f32[2048]{0:T(1024)S(1)}, f32[2048]{0:T(1024)S(1)}, u32[]{:S(2)}, u32[]{:S(2)}) collective-permute-start(f32[2048]{0:T(1024)S(1)} %broadcast_select_fusion.52), channel_id=1, source_target_pairs={{0,64},{64,0},{2,66},{66,2},{4,68},{68,4},{6,70},{70,6},{8,72},{72... | collective-permute-start | bytes 24584 | tf_op jit(solution)/shard_map/ppermute | solution.py:16
  91.3 15.5 %collective-permute-start.50 = (f32[2048]{0:T(1024)S(1)}, f32[2048]{0:T(1024)S(1)}, u32[]{:S(2)}, u32[]{:S(2)}) collective-permute-start(f32[2048]{0:T(1024)S(1)} %broadcast_select_fusion.69), channel_id=1, source_target_pairs={{0,128},{128,0},{2,130},{130,2},{4,132},{132,4},{6,134},{134,6},{8... | collective-permute-start | bytes 24584 | tf_op jit(solution)/shard_map/ppermute | solution.py:16
  95.6 43.3 %collective-permute-start.10 = (f32[3,2048]{1,0:T(4,128)S(1)}, f32[3,2048]{1,0:T(4,128)S(1)}, u32[]{:S(2)}, u32[]{:S(2)}) collective-permute-start(f32[3,2048]{1,0:T(4,128)S(1)} %broadcast_select_fusion.41), channel_id=1, source_target_pairs={{0,8},{8,0},{2,10},{10,2},{4,12},{12,4},{6,14},{14,6},{16,24},{24,... | collective-permute-start | bytes 73736 | tf_op jit(solution)/shard_map/ppermute | solution.py:16
  98.5 12.5 %collective-permute-start.57 = (f32[2048]{0:T(1024)S(1)}, f32[2048]{0:T(1024)S(1)}, u32[]{:S(2)}, u32[]{:S(2)}) collective-permute-start(f32[2048]{0:T(1024)S(1)} %broadcast_select_fusion.61), channel_id=1, source_target_pairs={{0,128},{128,0},{2,130},{130,2},{4,132},{132,4},{6,134},{134,6},{8... | collective-permute-start | bytes 24584 | tf_op jit(solution)/shard_map/ppermute | solution.py:16
  100.5 40.6 %collective-permute-start.24 = (f32[3,2048]{1,0:T(4,128)S(1)}, f32[3,2048]{1,0:T(4,128)S(1)}, u32[]{:S(2)}, u32[]{:S(2)}) collective-permute-start(f32[3,2048]{1,0:T(4,128)S(1)} %broadcast_select_fusion.33), channel_id=1, source_target_pairs={{0,8},{8,0},{2,10},{10,2},{4,12},{12,4},{6,14},{14,6},{16,24},{24,... | collective-permute-start | bytes 73736 | tf_op jit(solution)/shard_map/ppermute | solution.py:16
  106.8 7.2 %collective-permute-start.64 = (f32[2048]{0:T(1024)S(1)}, f32[2048]{0:T(1024)S(1)}, u32[]{:S(2)}, u32[]{:S(2)}) collective-permute-start(f32[2048]{0:T(1024)S(1)} %broadcast_select_fusion.53), channel_id=1, source_target_pairs={{0,128},{128,0},{2,130},{130,2},{4,132},{132,4},{6,134},{134,6},{8... | collective-permute-start | bytes 24584 | tf_op jit(solution)/shard_map/ppermute | solution.py:16
  111.1 33.2 %collective-permute-start.38 = (f32[3,2048]{1,0:T(4,128)S(1)}, f32[3,2048]{1,0:T(4,128)S(1)}, u32[]{:S(2)}, u32[]{:S(2)}) collective-permute-start(f32[3,2048]{1,0:T(4,128)S(1)} %broadcast_select_fusion.25), channel_id=1, source_target_pairs={{0,8},{8,0},{2,10},{10,2},{4,12},{12,4},{6,14},{14,6},{16,24},{24,... | collective-permute-start | bytes 73736 | tf_op jit(solution)/shard_map/ppermute | solution.py:16
  114.0 8.3 %collective-permute-start.51 = (f32[2048]{0:T(1024)S(1)}, f32[2048]{0:T(1024)S(1)}, u32[]{:S(2)}, u32[]{:S(2)}) collective-permute-start(f32[2048]{0:T(1024)S(1)} %broadcast_select_fusion.70), channel_id=1, source_target_pairs={{0,256},{256,0},{2,258},{258,2},{4,260},{260,4},{6,262},{262,6},{8... | collective-permute-start | bytes 24584 | tf_op jit(solution)/shard_map/ppermute | solution.py:16
  122.3 8.3 %collective-permute-start.58 = (f32[2048]{0:T(1024)S(1)}, f32[2048]{0:T(1024)S(1)}, u32[]{:S(2)}, u32[]{:S(2)}) collective-permute-start(f32[2048]{0:T(1024)S(1)} %broadcast_select_fusion.62), channel_id=1, source_target_pairs={{0,256},{256,0},{2,258},{258,2},{4,260},{260,4},{6,262},{262,6},{8... | collective-permute-start | bytes 24584 | tf_op jit(solution)/shard_map/ppermute | solution.py:16
  130.6 8.3 %collective-permute-start.65 = (f32[2048]{0:T(1024)S(1)}, f32[2048]{0:T(1024)S(1)}, u32[]{:S(2)}, u32[]{:S(2)}) collective-permute-start(f32[2048]{0:T(1024)S(1)} %broadcast_select_fusion.54), channel_id=1, source_target_pairs={{0,256},{256,0},{2,258},{258,2},{4,260},{260,4},{6,262},{262,6},{8... | collective-permute-start | bytes 24584 | tf_op jit(solution)/shard_map/ppermute | solution.py:16
  139.0 7.5 %collective-permute-start.11 = (f32[3,2048]{1,0:T(4,128)S(1)}, f32[3,2048]{1,0:T(4,128)S(1)}, u32[]{:S(2)}, u32[]{:S(2)}) collective-permute-start(f32[3,2048]{1,0:T(4,128)S(1)} %broadcast_select_fusion.42), channel_id=1, source_target_pairs={{0,16},{16,0},{2,18},{18,2},{4,20},{20,4},{6,22},{22,6},{8,24},{24... | collective-permute-start | bytes 73736 | tf_op jit(solution)/shard_map/ppermute | solution.py:16
  141.2 10.0 %collective-permute-start.25 = (f32[3,2048]{1,0:T(4,128)S(1)}, f32[3,2048]{1,0:T(4,128)S(1)}, u32[]{:S(2)}, u32[]{:S(2)}) collective-permute-start(f32[3,2048]{1,0:T(4,128)S(1)} %broadcast_select_fusion.34), channel_id=1, source_target_pairs={{0,16},{16,0},{2,18},{18,2},{4,20},{20,4},{6,22},{22,6},{8,24},{24... | collective-permute-start | bytes 73736 | tf_op jit(solution)/shard_map/ppermute | solution.py:16
  144.3 9.0 %collective-permute-start.39 = (f32[3,2048]{1,0:T(4,128)S(1)}, f32[3,2048]{1,0:T(4,128)S(1)}, u32[]{:S(2)}, u32[]{:S(2)}) collective-permute-start(f32[3,2048]{1,0:T(4,128)S(1)} %broadcast_select_fusion.26), channel_id=1, source_target_pairs={{0,16},{16,0},{2,18},{18,2},{4,20},{20,4},{6,22},{22,6},{8,24},{24... | collective-permute-start | bytes 73736 | tf_op jit(solution)/shard_map/ppermute | solution.py:16
  146.5 11.5 %collective-permute-start.12 = (f32[3,2048]{1,0:T(4,128)S(1)}, f32[3,2048]{1,0:T(4,128)S(1)}, u32[]{:S(2)}, u32[]{:S(2)}) collective-permute-start(f32[3,2048]{1,0:T(4,128)S(1)} %broadcast_select_fusion.43), channel_id=1, source_target_pairs={{0,32},{32,0},{2,34},{34,2},{4,36},{36,4},{6,38},{38,6},{8,40},{40... | collective-permute-start | bytes 73736 | tf_op jit(solution)/shard_map/ppermute | solution.py:16
  151.2 9.0 %collective-permute-start.26 = (f32[3,2048]{1,0:T(4,128)S(1)}, f32[3,2048]{1,0:T(4,128)S(1)}, u32[]{:S(2)}, u32[]{:S(2)}) collective-permute-start(f32[3,2048]{1,0:T(4,128)S(1)} %broadcast_select_fusion.35), channel_id=1, source_target_pairs={{0,32},{32,0},{2,34},{34,2},{4,36},{36,4},{6,38},{38,6},{8,40},{40... | collective-permute-start | bytes 73736 | tf_op jit(solution)/shard_map/ppermute | solution.py:16
  153.4 10.0 %collective-permute-start.40 = (f32[3,2048]{1,0:T(4,128)S(1)}, f32[3,2048]{1,0:T(4,128)S(1)}, u32[]{:S(2)}, u32[]{:S(2)}) collective-permute-start(f32[3,2048]{1,0:T(4,128)S(1)} %broadcast_select_fusion.27), channel_id=1, source_target_pairs={{0,32},{32,0},{2,34},{34,2},{4,36},{36,4},{6,38},{38,6},{8,40},{40... | collective-permute-start | bytes 73736 | tf_op jit(solution)/shard_map/ppermute | solution.py:16
  158.1 7.4 %collective-permute-start.13 = (f32[3,2048]{1,0:T(4,128)S(1)}, f32[3,2048]{1,0:T(4,128)S(1)}, u32[]{:S(2)}, u32[]{:S(2)}) collective-permute-start(f32[3,2048]{1,0:T(4,128)S(1)} %broadcast_select_fusion.44), channel_id=1, source_target_pairs={{0,64},{64,0},{2,66},{66,2},{4,68},{68,4},{6,70},{70,6},{8,72},{72... | collective-permute-start | bytes 73736 | tf_op jit(solution)/shard_map/ppermute | solution.py:16
  160.2 7.7 %collective-permute-start.27 = (f32[3,2048]{1,0:T(4,128)S(1)}, f32[3,2048]{1,0:T(4,128)S(1)}, u32[]{:S(2)}, u32[]{:S(2)}) collective-permute-start(f32[3,2048]{1,0:T(4,128)S(1)} %broadcast_select_fusion.36), channel_id=1, source_target_pairs={{0,64},{64,0},{2,66},{66,2},{4,68},{68,4},{6,70},{70,6},{8,72},{72... | collective-permute-start | bytes 73736 | tf_op jit(solution)/shard_map/ppermute | solution.py:16
  163.4 8.3 %collective-permute-start.41 = (f32[3,2048]{1,0:T(4,128)S(1)}, f32[3,2048]{1,0:T(4,128)S(1)}, u32[]{:S(2)}, u32[]{:S(2)}) collective-permute-start(f32[3,2048]{1,0:T(4,128)S(1)} %broadcast_select_fusion.28), channel_id=1, source_target_pairs={{0,64},{64,0},{2,66},{66,2},{4,68},{68,4},{6,70},{70,6},{8,72},{72... | collective-permute-start | bytes 73736 | tf_op jit(solution)/shard_map/ppermute | solution.py:16
  165.5 8.6 %collective-permute-start.14 = (f32[3,2048]{1,0:T(4,128)S(1)}, f32[3,2048]{1,0:T(4,128)S(1)}, u32[]{:S(2)}, u32[]{:S(2)}) collective-permute-start(f32[3,2048]{1,0:T(4,128)S(1)} %broadcast_select_fusion.45), channel_id=1, source_target_pairs={{0,128},{128,0},{2,130},{130,2},{4,132},{132,4},{6,134},{134,6},{8... | collective-permute-start | bytes 73736 | tf_op jit(solution)/shard_map/ppermute | solution.py:16
  167.9 13.4 %collective-permute-start.28 = (f32[3,2048]{1,0:T(4,128)S(1)}, f32[3,2048]{1,0:T(4,128)S(1)}, u32[]{:S(2)}, u32[]{:S(2)}) collective-permute-start(f32[3,2048]{1,0:T(4,128)S(1)} %broadcast_select_fusion.37), channel_id=1, source_target_pairs={{0,128},{128,0},{2,130},{130,2},{4,132},{132,4},{6,134},{134,6},{8... | collective-permute-start | bytes 73736 | tf_op jit(solution)/shard_map/ppermute | solution.py:16
  171.8 11.6 %collective-permute-start.42 = (f32[3,2048]{1,0:T(4,128)S(1)}, f32[3,2048]{1,0:T(4,128)S(1)}, u32[]{:S(2)}, u32[]{:S(2)}) collective-permute-start(f32[3,2048]{1,0:T(4,128)S(1)} %broadcast_select_fusion.29), channel_id=1, source_target_pairs={{0,128},{128,0},{2,130},{130,2},{4,132},{132,4},{6,134},{134,6},{8... | collective-permute-start | bytes 73736 | tf_op jit(solution)/shard_map/ppermute | solution.py:16
  174.1 16.6 %collective-permute-start.15 = (f32[3,2048]{1,0:T(4,128)S(1)}, f32[3,2048]{1,0:T(4,128)S(1)}, u32[]{:S(2)}, u32[]{:S(2)}) collective-permute-start(f32[3,2048]{1,0:T(4,128)S(1)} %broadcast_select_fusion.46), channel_id=1, source_target_pairs={{0,256},{256,0},{2,258},{258,2},{4,260},{260,4},{6,262},{262,6},{8... | collective-permute-start | bytes 73736 | tf_op jit(solution)/shard_map/ppermute | solution.py:16
  181.3 9.5 %collective-permute-start.29 = (f32[3,2048]{1,0:T(4,128)S(1)}, f32[3,2048]{1,0:T(4,128)S(1)}, u32[]{:S(2)}, u32[]{:S(2)}) collective-permute-start(f32[3,2048]{1,0:T(4,128)S(1)} %broadcast_select_fusion.38), channel_id=1, source_target_pairs={{0,256},{256,0},{2,258},{258,2},{4,260},{260,4},{6,262},{262,6},{8... | collective-permute-start | bytes 73736 | tf_op jit(solution)/shard_map/ppermute | solution.py:16
  183.4 8.7 %collective-permute-start.43 = (f32[3,2048]{1,0:T(4,128)S(1)}, f32[3,2048]{1,0:T(4,128)S(1)}, u32[]{:S(2)}, u32[]{:S(2)}) collective-permute-start(f32[3,2048]{1,0:T(4,128)S(1)} %broadcast_select_fusion.30), channel_id=1, source_target_pairs={{0,256},{256,0},{2,258},{258,2},{4,260},{260,4},{6,262},{262,6},{8... | collective-permute-start | bytes 73736 | tf_op jit(solution)/shard_map/ppermute | solution.py:16
  253.7 27.1 %collective-permute-start.1 = (f32[32,2048]{1,0:T(8,128)S(1)}, f32[32,2048]{1,0:T(8,128)S(1)}, u32[]{:S(2)}, u32[]{:S(2)}) collective-permute-start(f32[32,2048]{1,0:T(8,128)S(1)} %get-tuple-element.17), channel_id=1, source_target_pairs={{0,4},{4,0},{2,6},{6,2},{8,12},{12,8},{10,14},{14,10},{16,20},{20,... | collective-permute-start | bytes 786440 | tf_op jit(solution)/shard_map/ppermute | solution.py:16
  274.5 20.5 %collective-permute-start.16 = (f32[32,2048]{1,0:T(8,128)S(1)}, f32[32,2048]{1,0:T(8,128)S(1)}, u32[]{:S(2)}, u32[]{:S(2)}) collective-permute-start(f32[32,2048]{1,0:T(8,128)S(1)} %get-tuple-element.16), channel_id=1, source_target_pairs={{0,4},{4,0},{2,6},{6,2},{8,12},{12,8},{10,14},{14,10},{16,20},{20,... | collective-permute-start | bytes 786440 | tf_op jit(solution)/shard_map/ppermute | solution.py:16
  276.7 23.7 %collective-permute-start.30 = (f32[32,2048]{1,0:T(8,128)S(1)}, f32[32,2048]{1,0:T(8,128)S(1)}, u32[]{:S(2)}, u32[]{:S(2)}) collective-permute-start(f32[32,2048]{1,0:T(8,128)S(1)} %get-tuple-element.15), channel_id=1, source_target_pairs={{0,4},{4,0},{2,6},{6,2},{8,12},{12,8},{10,14},{14,10},{16,20},{20,... | collective-permute-start | bytes 786440 | tf_op jit(solution)/shard_map/ppermute | solution.py:16
  280.8 23.5 %collective-permute-start.2 = (f32[32,2048]{1,0:T(8,128)S(1)}, f32[32,2048]{1,0:T(8,128)S(1)}, u32[]{:S(2)}, u32[]{:S(2)}) collective-permute-start(f32[32,2048]{1,0:T(8,128)S(1)} %broadcast_select_fusion.17), channel_id=1, source_target_pairs={{0,8},{8,0},{2,10},{10,2},{4,12},{12,4},{6,14},{14,6},{16,24},{24,... | collective-permute-start | bytes 786440 | tf_op jit(solution)/shard_map/ppermute | solution.py:16
  295.0 21.5 %collective-permute-start.17 = (f32[32,2048]{1,0:T(8,128)S(1)}, f32[32,2048]{1,0:T(8,128)S(1)}, u32[]{:S(2)}, u32[]{:S(2)}) collective-permute-start(f32[32,2048]{1,0:T(8,128)S(1)} %broadcast_select_fusion.9), channel_id=1, source_target_pairs={{0,8},{8,0},{2,10},{10,2},{4,12},{12,4},{6,14},{14,6},{16,24},{24,... | collective-permute-start | bytes 786440 | tf_op jit(solution)/shard_map/ppermute | solution.py:16
  300.4 22.1 %collective-permute-start.31 = (f32[32,2048]{1,0:T(8,128)S(1)}, f32[32,2048]{1,0:T(8,128)S(1)}, u32[]{:S(2)}, u32[]{:S(2)}) collective-permute-start(f32[32,2048]{1,0:T(8,128)S(1)} %broadcast_select_fusion.1), channel_id=1, source_target_pairs={{0,8},{8,0},{2,10},{10,2},{4,12},{12,4},{6,14},{14,6},{16,24},{24,... | collective-permute-start | bytes 786440 | tf_op jit(solution)/shard_map/ppermute | solution.py:16
  304.3 21.8 %collective-permute-start.3 = (f32[32,2048]{1,0:T(8,128)S(1)}, f32[32,2048]{1,0:T(8,128)S(1)}, u32[]{:S(2)}, u32[]{:S(2)}) collective-permute-start(f32[32,2048]{1,0:T(8,128)S(1)} %broadcast_select_fusion.18), channel_id=1, source_target_pairs={{0,16},{16,0},{2,18},{18,2},{4,20},{20,4},{6,22},{22,6},{8,24},{24... | collective-permute-start | bytes 786440 | tf_op jit(solution)/shard_map/ppermute | solution.py:16
  316.6 11.9 %collective-permute-start.18 = (f32[32,2048]{1,0:T(8,128)S(1)}, f32[32,2048]{1,0:T(8,128)S(1)}, u32[]{:S(2)}, u32[]{:S(2)}) collective-permute-start(f32[32,2048]{1,0:T(8,128)S(1)} %broadcast_select_fusion.10), channel_id=1, source_target_pairs={{0,16},{16,0},{2,18},{18,2},{4,20},{20,4},{6,22},{22,6},{8,24},{24... | collective-permute-start | bytes 786440 | tf_op jit(solution)/shard_map/ppermute | solution.py:16
  322.6 10.5 %collective-permute-start.32 = (f32[32,2048]{1,0:T(8,128)S(1)}, f32[32,2048]{1,0:T(8,128)S(1)}, u32[]{:S(2)}, u32[]{:S(2)}) collective-permute-start(f32[32,2048]{1,0:T(8,128)S(1)} %broadcast_select_fusion.2), channel_id=1, source_target_pairs={{0,16},{16,0},{2,18},{18,2},{4,20},{20,4},{6,22},{22,6},{8,24},{24... | collective-permute-start | bytes 786440 | tf_op jit(solution)/shard_map/ppermute | solution.py:16
  326.2 11.3 %collective-permute-start.4 = (f32[32,2048]{1,0:T(8,128)S(1)}, f32[32,2048]{1,0:T(8,128)S(1)}, u32[]{:S(2)}, u32[]{:S(2)}) collective-permute-start(f32[32,2048]{1,0:T(8,128)S(1)} %broadcast_select_fusion.19), channel_id=1, source_target_pairs={{0,32},{32,0},{2,34},{34,2},{4,36},{36,4},{6,38},{38,6},{8,40},{40... | collective-permute-start | bytes 786440 | tf_op jit(solution)/shard_map/ppermute | solution.py:16
  328.5 14.6 %collective-permute-start.19 = (f32[32,2048]{1,0:T(8,128)S(1)}, f32[32,2048]{1,0:T(8,128)S(1)}, u32[]{:S(2)}, u32[]{:S(2)}) collective-permute-start(f32[32,2048]{1,0:T(8,128)S(1)} %broadcast_select_fusion.11), channel_id=1, source_target_pairs={{0,32},{32,0},{2,34},{34,2},{4,36},{36,4},{6,38},{38,6},{8,40},{40... | collective-permute-start | bytes 786440 | tf_op jit(solution)/shard_map/ppermute | solution.py:16
  333.1 15.6 %collective-permute-start.33 = (f32[32,2048]{1,0:T(8,128)S(1)}, f32[32,2048]{1,0:T(8,128)S(1)}, u32[]{:S(2)}, u32[]{:S(2)}) collective-permute-start(f32[32,2048]{1,0:T(8,128)S(1)} %broadcast_select_fusion.3), channel_id=1, source_target_pairs={{0,32},{32,0},{2,34},{34,2},{4,36},{36,4},{6,38},{38,6},{8,40},{40... | collective-permute-start | bytes 786440 | tf_op jit(solution)/shard_map/ppermute | solution.py:16
  337.5 14.6 %collective-permute-start.5 = (f32[32,2048]{1,0:T(8,128)S(1)}, f32[32,2048]{1,0:T(8,128)S(1)}, u32[]{:S(2)}, u32[]{:S(2)}) collective-permute-start(f32[32,2048]{1,0:T(8,128)S(1)} %broadcast_select_fusion.20), channel_id=1, source_target_pairs={{0,64},{64,0},{2,66},{66,2},{4,68},{68,4},{6,70},{70,6},{8,72},{72... | collective-permute-start | bytes 786440 | tf_op jit(solution)/shard_map/ppermute | solution.py:16
  343.1 13.8 %collective-permute-start.20 = (f32[32,2048]{1,0:T(8,128)S(1)}, f32[32,2048]{1,0:T(8,128)S(1)}, u32[]{:S(2)}, u32[]{:S(2)}) collective-permute-start(f32[32,2048]{1,0:T(8,128)S(1)} %broadcast_select_fusion.12), channel_id=1, source_target_pairs={{0,64},{64,0},{2,66},{66,2},{4,68},{68,4},{6,70},{70,6},{8,72},{72... | collective-permute-start | bytes 786440 | tf_op jit(solution)/shard_map/ppermute | solution.py:16
  348.8 10.2 %collective-permute-start.34 = (f32[32,2048]{1,0:T(8,128)S(1)}, f32[32,2048]{1,0:T(8,128)S(1)}, u32[]{:S(2)}, u32[]{:S(2)}) collective-permute-start(f32[32,2048]{1,0:T(8,128)S(1)} %broadcast_select_fusion.4), channel_id=1, source_target_pairs={{0,64},{64,0},{2,66},{66,2},{4,68},{68,4},{6,70},{70,6},{8,72},{72... | collective-permute-start | bytes 786440 | tf_op jit(solution)/shard_map/ppermute | solution.py:16
  352.2 11.2 %collective-permute-start.6 = (f32[32,2048]{1,0:T(8,128)S(1)}, f32[32,2048]{1,0:T(8,128)S(1)}, u32[]{:S(2)}, u32[]{:S(2)}) collective-permute-start(f32[32,2048]{1,0:T(8,128)S(1)} %broadcast_select_fusion.21), channel_id=1, source_target_pairs={{0,128},{128,0},{2,130},{130,2},{4,132},{132,4},{6,134},{134,6},{8... | collective-permute-start | bytes 786440 | tf_op jit(solution)/shard_map/ppermute | solution.py:16
  357.0 14.7 %collective-permute-start.21 = (f32[32,2048]{1,0:T(8,128)S(1)}, f32[32,2048]{1,0:T(8,128)S(1)}, u32[]{:S(2)}, u32[]{:S(2)}) collective-permute-start(f32[32,2048]{1,0:T(8,128)S(1)} %broadcast_select_fusion.13), channel_id=1, source_target_pairs={{0,128},{128,0},{2,130},{130,2},{4,132},{132,4},{6,134},{134,6},{8... | collective-permute-start | bytes 786440 | tf_op jit(solution)/shard_map/ppermute | solution.py:16
  359.0 38.6 %collective-permute-start.35 = (f32[32,2048]{1,0:T(8,128)S(1)}, f32[32,2048]{1,0:T(8,128)S(1)}, u32[]{:S(2)}, u32[]{:S(2)}) collective-permute-start(f32[32,2048]{1,0:T(8,128)S(1)} %broadcast_select_fusion.5), channel_id=1, source_target_pairs={{0,128},{128,0},{2,130},{130,2},{4,132},{132,4},{6,134},{134,6},{8... | collective-permute-start | bytes 786440 | tf_op jit(solution)/shard_map/ppermute | solution.py:16
  363.4 41.3 %collective-permute-start.7 = (f32[32,2048]{1,0:T(8,128)S(1)}, f32[32,2048]{1,0:T(8,128)S(1)}, u32[]{:S(2)}, u32[]{:S(2)}) collective-permute-start(f32[32,2048]{1,0:T(8,128)S(1)} %broadcast_select_fusion.22), channel_id=1, source_target_pairs={{0,256},{256,0},{2,258},{258,2},{4,260},{260,4},{6,262},{262,6},{8... | collective-permute-start | bytes 786440 | tf_op jit(solution)/shard_map/ppermute | solution.py:16
  371.7 58.9 %collective-permute-start.22 = (f32[32,2048]{1,0:T(8,128)S(1)}, f32[32,2048]{1,0:T(8,128)S(1)}, u32[]{:S(2)}, u32[]{:S(2)}) collective-permute-start(f32[32,2048]{1,0:T(8,128)S(1)} %broadcast_select_fusion.14), channel_id=1, source_target_pairs={{0,256},{256,0},{2,258},{258,2},{4,260},{260,4},{6,262},{262,6},{8... | collective-permute-start | bytes 786440 | tf_op jit(solution)/shard_map/ppermute | solution.py:16
  397.6 59.2 %collective-permute-start.36 = (f32[32,2048]{1,0:T(8,128)S(1)}, f32[32,2048]{1,0:T(8,128)S(1)}, u32[]{:S(2)}, u32[]{:S(2)}) collective-permute-start(f32[32,2048]{1,0:T(8,128)S(1)} %broadcast_select_fusion.6), channel_id=1, source_target_pairs={{0,256},{256,0},{2,258},{258,2},{4,260},{260,4},{6,262},{262,6},{8... | collective-permute-start | bytes 786440 | tf_op jit(solution)/shard_map/ppermute | solution.py:16
  (15 other events, 1290.6 us)
where the time goes:
time: 719 us; the launch traced here: 705 us
  starting transfers between devices  253 us (35%)
  matrix products  231 us (32%)
  blocking collectives  138 us (19%)
  waiting for transfers between devices  61.1 us (8%)
  between operations  12.5 us (2%)
    ppermute x66, starting transfers between devices, from_partner(): return lax.ppermute(block, axis, route)  253 us
    dot_general x19, matrix products, hdot(): jnp.dot(left, right, precision=lax.Precision.HIGHEST, preferred_element_t...  231 us
    psum x1, blocking collectives, local(): quad_total = quad_total + lax.psum(quad_round * quad_weight, ('blk', 'pr'))  138 us
    ppermute x66, waiting for transfers between devices, from_partner(): return lax.ppermute(block, axis, route)  61.1 us
  transfers between devices with their start and end apart: 66, of which 15 were waited for; matrix products, arithmetic and copies ran while one was open for 19% of the time, Pallas kernels for 0%

commit v1 on v0

v1 whole, which is shorter than its diff:
```python
import math
import jax
import jax.numpy as jnp
from jax import lax
from jax.experimental import pallas as pl
from jax.experimental.pallas import tpu as pltpu
from jax.sharding import PartitionSpec as P

F32, BF16 = jnp.float32, jnp.bfloat16
MESH = pl.DeviceIdType.MESH
ROUNDS = 3
COLS = 2048
HALF = 1024
TB = 512
TA = 256
STRIP = 16


def split(value):
    hi = value.astype(BF16)
    return hi, (value - hi.astype(F32)).astype(BF16)


def tile_terms(xa, xb, ka, kb, k2):
    d2 = None
    for comp in range(3):
        off = xa[:, comp:comp + 1] - xb[comp]
        d2 = off * off if d2 is None else d2 + off * off
    dist = d2 * lax.rsqrt(jnp.maximum(d2, 1e-30))
    decay = jnp.exp2(dist * ka)
    bell = (1.0 + dist * kb) * decay
    return bell + (d2 * k2) * decay, d2 * bell


def whole(ref, sem):
    pltpu.make_async_copy(ref, ref, sem).wait()


def body(
    plan, pick, cst, coords, alpha, probes, solves,
    kz_out, dkz_out, grad_out,
    comps, buf_a, buf_ac, st_a, st_ac, buf_b, buf_bc, buf_c0, buf_c1, buf_c2, buf_cc, st_b, st_bc, p32, payc,
    picked, plhs, xat, khi, klo, shi, slo, acc_k, acc_s, buf_r, sc1, buf_s1, sc2, buf_s2,
    s_a1, r_a1, s_a2, r_a2, s_b1, r_b1, s_b2, r_b2, s_r, r_r, s_s, r_s,
):
    buf_c = (buf_c0, buf_c1, buf_c2)
    blk = lax.axis_index("blk")
    half = lax.axis_index("pr")
    core = blk % 2
    zhi = (blk // 2) % 4
    x = (blk // 8) % 4
    y = blk // 32
    m_a = y * 4 + zhi
    m_b = x * 2 + core
    a64 = half * 32 + m_a

    def dev_a(k):
        m = k % 32
        return {"blk": (((m // 4) * 4 + x) * 4 + m % 4) * 2 + core, "pr": k // 32}

    def dev_b(k):
        return {"blk": ((y * 4 + k // 2) * 4 + zhi) * 2 + k % 2, "pr": half}

    def send(src, dst, ssem, rsem, dev):
        pltpu.make_async_remote_copy(
            src_ref=src, dst_ref=dst, send_sem=ssem, recv_sem=rsem, device_id=dev, device_id_type=MESH
        ).start()

    shifts = [plan[r, 0] for r in range(ROUNDS)]
    t_a = [(s // 32) * 4 + (s // 2) % 4 for s in shifts]
    t_b = [((s // 8) % 4) * 2 + s % 2 for s in shifts]

    barrier = pltpu.get_barrier_semaphore()

    def greet_a(k, _):
        pl.semaphore_signal(barrier, inc=1, device_id=dev_a((a64 + k) % 64), device_id_type=MESH)
        return 0

    def greet_b(k, _):
        pl.semaphore_signal(barrier, inc=1, device_id=dev_b((m_b + k) % 8), device_id_type=MESH)
        return 0

    lax.fori_loop(1, 64, greet_a, 0)
    lax.fori_loop(1, 8, greet_b, 0)

    for g in range(4):
        row = coords[g:g + 1, :] if g < 3 else alpha[...]
        for t in range(16):
            comps[g, t] = row[:, t * 128:(t + 1) * 128]
    pl.semaphore_wait(barrier, 70)

    def probe_tile(hh, yy, zz):
        rows = pl.ds(pl.multiple_of(zz * 8, 8), 8)
        return rows, pl.ds(pl.multiple_of(hh * HALF + yy * 128, 128), 128)

    def spread_comps(k, _):
        m = (m_a + k) % 32
        send(comps.at[m % 4, half * 8 + m // 4], buf_ac.at[m_a], s_a1.at[0], r_a1.at[0], dev_a(half * 32 + m))
        return 0

    def spread_probes(k, _):
        d = (a64 + k) % 64
        m = d % 32
        rows, cols = probe_tile(d // 32, m // 4, m % 4)
        send(probes.at[rows, cols], buf_a.at[a64], s_a1.at[1], r_a1.at[1], dev_a(d))
        return 0

    lax.fori_loop(1, 32, spread_comps, 0)
    lax.fori_loop(1, 64, spread_probes, 0)
    buf_ac[m_a] = comps[zhi, half * 8 + y]
    rows, cols = probe_tile(half, y, zhi)
    buf_a[a64] = probes[rows, cols]

    for j in range(64):
        picked[j:j + 1, :] = solves[pl.ds(pick[j], 1), :]

    whole(buf_ac.at[0:31], r_a1.at[0])

    def select_ac(k, _):
        i = (m_a + k) % 32
        for r in range(ROUNDS):
            st_ac[i, r:r + 1, :] = buf_ac[i ^ t_a[r]]
        st_ac[i, 3:4, :] = jnp.zeros((1, 128), F32)
        send(st_ac.at[i], buf_bc.at[y, zhi], s_a2.at[3], r_a2.at[3], dev_a(half * 32 + i))
        return 0

    lax.fori_loop(1, 32, select_ac, 0)
    for r in range(ROUNDS):
        buf_bc[y, zhi, r:r + 1, :] = buf_ac[m_a ^ t_a[r]]
    buf_bc[y, zhi, 3:4, :] = jnp.zeros((1, 128), F32)

    whole(buf_a.at[0:63], r_a1.at[1])

    def select_a(r):
        def one(k, _):
            i = (m_a + k) % 32
            j = i ^ t_a[r]
            st_a[r, i, 0] = buf_a[j]
            st_a[r, i, 1] = buf_a[32 + j]
            send(st_a.at[r, i], buf_b.at[r, y, zhi], s_a2.at[r], r_a2.at[r], dev_a(half * 32 + i))
            return 0

        lax.fori_loop(1, 32, one, 0)
        j = m_a ^ t_a[r]
        buf_b[r, y, zhi, 0] = buf_a[j]
        buf_b[r, y, zhi, 1] = buf_a[32 + j]

    def spread_b(r):
        whole(st_a.at[r, 0:31], r_a2.at[r])

        def one(k, _):
            d = (m_b + k) % 8
            send(buf_b.at[r, d], buf_c[r].at[m_b], s_b1.at[r], r_b1.at[r], dev_b(d))
            return 0

        lax.fori_loop(1, 8, one, 0)
        buf_c[r][m_b] = buf_b[r, m_b]

    def select_b(r):
        whole(buf_c[r].at[0:7], r_b1.at[r])
        cols = pl.ds(pl.multiple_of(m_b * 128, 128), 128)

        def one(k, _):
            d = (m_b + k) % 8
            j = d ^ t_b[r]
            for hh in range(2):
                for g in range(4):
                    lo = (hh * 4 + g) * 8
                    st_b[r, d, lo:lo + 8, :] = buf_c[r][j, g, hh]
            send(st_b.at[r, d], p32.at[r, 0:64, cols], s_b2.at[r], r_b2.at[r], dev_b(d))
            return 0

        lax.fori_loop(1, 8, one, 0)
        j = m_b ^ t_b[r]
        for hh in range(2):
            for g in range(4):
                lo = (hh * 4 + g) * 8
                p32[r, lo:lo + 8, cols] = buf_c[r][j, g, hh]

    for r in range(ROUNDS):
        select_a(r)

    whole(st_ac.at[0:31], r_a2.at[3])

    def spread_bc(k, _):
        d = (m_b + k) % 8
        send(buf_bc.at[d], buf_cc.at[m_b], s_b1.at[3], r_b1.at[3], dev_b(d))
        return 0

    lax.fori_loop(1, 8, spread_bc, 0)
    buf_cc[m_b] = buf_bc[m_b]
    whole(buf_cc.at[0:7], r_b1.at[3])

    def select_bc(k, _):
        d = (m_b + k) % 8
        for r in range(ROUNDS):
            for g in range(4):
                st_bc[d, g, r:r + 1, :] = buf_cc[d ^ t_b[r], g, r:r + 1, :]
        for g in range(4):
            st_bc[d, g, 3:4, :] = jnp.zeros((1, 128), F32)
        send(st_bc.at[d], payc.at[m_b], s_b2.at[3], r_b2.at[3], dev_b(d))
        return 0

    lax.fori_loop(1, 8, select_bc, 0)
    for r in range(ROUNDS):
        for g in range(4):
            payc[m_b, g, r:r + 1, :] = buf_cc[m_b ^ t_b[r], g, r:r + 1, :]
    for r in range(ROUNDS):
        spread_b(r)
    whole(st_bc.at[0:7], r_b2.at[3])
    for r in range(ROUNDS):
        for t in range(8):
            for g in range(4):
                p32[r, 64 + g:65 + g, t * 128:(t + 1) * 128] = payc[t, g, r:r + 1, :]
        p32[r, 68:72, :] = jnp.zeros((4, HALF), F32)
    for r in range(ROUNDS):
        select_b(r)

    acc_k[...] = jnp.zeros_like(acc_k)
    acc_s[...] = jnp.zeros_like(acc_s)
    noise = jnp.sum(
        picked[pl.ds(pl.multiple_of(half * 32, 32), 32), :] * probes[...], axis=0, keepdims=True
    )
    own = alpha[...]
    noise = 0.5 * own * own - noise * (1.0 / 64.0)

    ka, kb, k2, k_slope = cst[0], cst[1], cst[2], cst[3]

    for r in range(ROUNDS):
        whole(st_b.at[r, 0:7], r_b2.at[r])
        p = jnp.concatenate([p32[r], jnp.zeros((8, HALF), F32)], 0)
        hi, lo = split(p)
        plhs[0:80, :] = hi
        plhs[80:160, :] = lo
        xat[...] = jnp.transpose(p32[r, 64:72, :])

        def step(t, _):
            b = pl.multiple_of(t * TB, TB)
            xb = [coords[c:c + 1, pl.ds(b, TB)] for c in range(3)]
            sum_k = sum_s = None
            for a in range(0, HALF, TA):
                for st in range(a, a + TA, STRIP):
                    kern, slope = tile_terms(xat[st:st + STRIP, :], xb, ka, kb, k2)
                    khi[st:st + STRIP, :], klo[st:st + STRIP, :] = split(kern)
                    shi[st:st + STRIP, :], slo[st:st + STRIP, :] = split(slope)
                lhs = plhs[:, a:a + TA]

                def product(hi, lo):
                    one = jnp.dot(lhs, hi[a:a + TA, :], preferred_element_type=F32)
                    two = jnp.dot(lhs[:80], lo[a:a + TA, :], preferred_element_type=F32)
                    return one[:72] + one[80:152] + two[:72]

                more_k, more_s = product(khi, klo), product(shi, slo)
                sum_k = more_k if sum_k is None else sum_k + more_k
                sum_s = more_s if sum_s is None else sum_s + more_s
            acc_k[:, pl.ds(b, TB)] += sum_k
            acc_s[:, pl.ds(b, TB)] += sum_s
            return 0

        lax.fori_loop(0, COLS // TB, step, 0)

    other = pl.ds(pl.multiple_of((1 - half) * 32, 32), 32)
    mine = pl.ds(pl.multiple_of(half * 32, 32), 32)
    mate = {"blk": blk, "pr": 1 - half}
    send(acc_k.at[other, :], buf_r.at[0], s_r.at[0], r_r.at[0], mate)
    send(acc_s.at[other, :], buf_r.at[1], s_r.at[1], r_r.at[1], mate)

    slope = acc_s[67:68, :] * own - jnp.sum(picked[...] * acc_s[0:64, :], axis=0, keepdims=True) * (1.0 / 64.0)
    slope = slope * k_slope
    rows_n, rows_s = noise[:, 0:128], slope[:, 0:128]
    for t in range(1, 16):
        rows_n = rows_n + noise[:, t * 128:(t + 1) * 128]
        rows_s = rows_s + slope[:, t * 128:(t + 1) * 128]
    sc1[0:1, :] = rows_n
    sc1[1:2, :] = rows_s

    def scalars_a(k, _):
        send(sc1, buf_s1.at[a64], s_s.at[0], r_s.at[0], dev_a((a64 + k) % 64))
        return 0

    lax.fori_loop(1, 64, scalars_a, 0)
    buf_s1[a64] = sc1[...]
    whole(buf_s1.at[0:63], r_s.at[0])
    sc2[...] = jnp.sum(buf_s1[...], axis=0)

    def scalars_b(k, _):
        send(sc2, buf_s2.at[m_b], s_s.at[1], r_s.at[1], dev_b((m_b + k) % 8))
        return 0

    lax.fori_loop(1, 8, scalars_b, 0)
    buf_s2[m_b] = sc2[...]

    whole(buf_r.at[0], r_r.at[0])
    kz_out[...] = acc_k[mine, :] + buf_r[0]
    whole(buf_r.at[1], r_r.at[1])
    dkz_out[...] = (acc_s[mine, :] + buf_r[1]) * k_slope

    whole(buf_s2.at[0:7], r_s.at[1])
    total = jnp.sum(jnp.sum(buf_s2[...], axis=0), axis=1, keepdims=True) * (0.5 / COLS)
    grad_out[...] = jnp.broadcast_to(total, (2, 128))

    whole(buf_ac.at[0:31], s_a1.at[0])
    whole(buf_a.at[0:63], s_a1.at[1])
    whole(st_ac.at[0:31], s_a2.at[3])
    whole(buf_cc.at[0:7], s_b1.at[3])
    whole(st_bc.at[0:7], s_b2.at[3])
    for r in range(ROUNDS):
        whole(st_a.at[r, 0:31], s_a2.at[r])
        whole(buf_c[r].at[0:7], s_b1.at[r])
        whole(st_b.at[r, 0:7], s_b2.at[r])
    whole(buf_r.at[0], s_r.at[0])
    whole(buf_r.at[1], s_r.at[1])
    whole(buf_s1.at[0:63], s_s.at[0])
    whole(buf_s2.at[0:7], s_s.at[1])


def local(coords, probes, solves, alpha, lengthscale, column_pick, plan):
    rate = math.sqrt(5.0) / lengthscale[0]
    cst = jnp.stack([
        rate * (-math.log2(math.e)), rate, rate * rate / 3.0, rate * rate / (3.0 * lengthscale[0])
    ])
    vm = pl.BlockSpec(memory_space=pltpu.VMEM)
    sm = pl.BlockSpec(memory_space=pltpu.SMEM)
    V, dma = pltpu.VMEM, pltpu.SemaphoreType.DMA
    kz, dkz, grad = pl.pallas_call(
        body,
        out_shape=[
            jax.ShapeDtypeStruct((32, COLS), F32),
            jax.ShapeDtypeStruct((32, COLS), F32),
            jax.ShapeDtypeStruct((2, 128), F32),
        ],
        in_specs=[sm, sm, sm, vm, vm, vm, vm],
        out_specs=[vm, vm, vm],
        scratch_shapes=[
            V((4, 16, 1, 128), F32),
            V((64, 8, 128), F32), V((32, 1, 128), F32),
            V((ROUNDS, 32, 2, 8, 128), F32), V((32, 4, 128), F32),
            V((ROUNDS, 8, 4, 2, 8, 128), F32), V((8, 4, 4, 128), F32),
            V((8, 4, 2, 8, 128), F32), V((8, 4, 2, 8, 128), F32), V((8, 4, 2, 8, 128), F32),
            V((8, 4, 4, 128), F32),
            V((ROUNDS, 8, 64, 128), F32), V((8, 4, 4, 128), F32),
            V((ROUNDS, 72, HALF), F32), V((8, 4, 4, 128), F32),
            V((64, COLS), F32),
            V((160, HALF), BF16), V((HALF, 8), F32),
            V((HALF, TB), BF16), V((HALF, TB), BF16), V((HALF, TB), BF16), V((HALF, TB), BF16),
            V((72, COLS), F32), V((72, COLS), F32),
            V((2, 32, COLS), F32),
            V((2, 128), F32), V((64, 2, 128), F32), V((2, 128), F32), V((8, 2, 128), F32),
            dma((2,)), dma((2,)),
            dma((4,)), dma((4,)),
            dma((4,)), dma((4,)),
            dma((4,)), dma((4,)),
            dma((2,)), dma((2,)),
            dma((2,)), dma((2,)),
        ],
        compiler_params=pltpu.CompilerParams(
            collective_id=0, has_side_effects=True, vmem_limit_bytes=40 * 2 ** 20
        ),
    )(plan, column_pick, cst, coords, alpha.reshape(1, COLS), probes, solves)
    return kz, dkz, grad[:, 0]


def solution(mesh):
    placed = (P(None, "blk"), P("pr", "blk"), P(None, "blk"), P("blk"), P(), P(), P())
    return jax.shard_map(
        local,
        mesh=mesh,
        in_specs=placed,
        out_specs=(P("pr", "blk"), P("pr", "blk"), P()),
        check_vma=False,
    )
```

time: 719 us -> 118 us (0.16); the launches traced: 705 us -> 117 us
  starting transfers between devices: 253 us -> 0 us
  matrix products: 231 us -> 0 us
  blocking collectives: 138 us -> 0 us
  Pallas kernels: 0 us -> 111 us
  waiting for transfers between devices: 61.1 us -> 0 us
  between operations: 12.5 us -> 1.39 us
    ppermute x66 -> x0, starting transfers between devices: 253 us -> none  [from_partner(): return lax.ppermute(block, axis, route)]
    dot_general x19 -> x0, matrix products: 231 us -> none  [hdot(): jnp.dot(left, right, precision=lax.Precision.HIGHEST, preferred_element_t...]
    psum x1 -> x0, blocking collectives: 138 us -> none  [local(): quad_total = quad_total + lax.psum(quad_round * quad_weight, ('blk', 'pr'))]
    pallas_call x0 -> x1, Pallas kernels: none -> 111 us  [local(): pl.pallas_call(body, out_shape=[jax.ShapeDtypeStruct((32, COLS), F32), ja...]
    ppermute x66 -> x0, waiting for transfers between devices: 61.1 us -> none  [from_partner(): return lax.ppermute(block, axis, route)]
  transfers between devices with their start and end apart: 66 -> 0, of which waited for: 15 -> 0; matrix products, arithmetic and copies ran while one was open for 19% -> 0% of each run, Pallas kernels for 0% -> 0%
where the time goes in v1:
time: 118 us; the launch traced here: 117 us
  Pallas kernels  111 us (94%)
  local copies, waits for them, and re-layouts  5.44 us (5%)
  between operations  1.39 us (1%)
    pallas_call x1, Pallas kernels, local(): pl.pallas_call(body, out_shape=[jax.ShapeDtypeStruct((32, COLS), F32), ja...  111 us
    unnamed x14, local copies, waits for them, and re-layouts  4.81 us

profile of v1, /device:TPU:1, one launch (start us, length us, event | category | flops | bytes accessed | tf_op | source)
XLA Modules:
  0.0 117.5 jit_solution(9610847413632335696)
XLA Ops:
  1.3 0.0 copy-start.3
  1.4 0.0 copy-start.4
  1.4 0.1 pad_maximum_fusion.cst
  1.5 0.0 copy-start.5
  1.5 0.5 copy-done.3
  2.0 0.1 copy-done.4
  2.1 0.1 copy-done.5
  2.1 0.0 copy-start
  2.1 1.0 copy-done
  3.2 0.0 copy-start.1
  3.2 0.9 copy-done.1
  4.1 0.0 copy-start.2
  4.1 0.8 copy-done.2
  4.9 110.6 %shard_map.94 = (f32[32,2048]{1,0:T(8,128)S(1)}, f32[32,2048]{1,0:T(8,128)S(1)}, f32[2,128]{1,0:T(2,128)S(1)}) custom-call(s32[3,256]{1,0:T(4,128)S(1)} %copy-done.4, s32[64]{0:T(128)S(1)} %copy-done.5, f32[4]{0:T(128)S(1)} %pad_maximum_fusion.cst, f32[3,2048]{1,0:T(4,128)S(1)} %copy-done.2, f32[1,2048]{1,0:T(1,128)S(1)} %bitcast.1, ...), custom_call_target="tpu_custom_call" | custom-call | tf_op jit(solution)/shard_map/pallas_call | solution.py:325
  115.5 0.6 slice_reduce_fusion
  116.1 0.7 copy.13
  116.8 0.7 copy.14
Async XLA Ops:
  1.3 0.7 copy-start.3
  1.4 0.7 copy-start.4
  1.5 0.7 copy-start.5
  2.1 1.0 copy-start
  3.2 0.9 copy-start.1
  4.1 0.8 copy-start.2

commit v2 on v1

v2 whole, which is shorter than its diff:
```python
import math
import jax
import jax.numpy as jnp
from jax import lax
from jax.experimental import pallas as pl
from jax.experimental.pallas import tpu as pltpu
from jax.sharding import PartitionSpec as P

F32, BF16 = jnp.float32, jnp.bfloat16
MESH = pl.DeviceIdType.MESH
ROUNDS = 3
COLS = 2048
HALF = 1024
TB = 512
TA = 256
STRIP = 16
STEPS = COLS // TB


def split(value):
    hi = value.astype(BF16)
    return hi, (value - hi.astype(F32)).astype(BF16)


def tile_terms(xa, xb, ka, kb, k2):
    d2 = None
    for comp in range(3):
        off = xa[:, comp:comp + 1] - xb[comp]
        d2 = off * off if d2 is None else d2 + off * off
    dist = d2 * lax.rsqrt(jnp.maximum(d2, 1e-30))
    decay = jnp.exp2(dist * ka)
    bell = (1.0 + dist * kb) * decay
    return bell + (d2 * k2) * decay, d2 * bell


def whole(ref, sem):
    pltpu.make_async_copy(ref, ref, sem).wait()


def body(
    plan, pick, cst, coords_h, alpha_h, probes_h, solves_h,
    kz_out, dkz_out, grad_out,
    coords, alpha, probes, solves,
    comps, buf_a, buf_ac, st_a, st_ac, buf_b, buf_bc, buf_c0, buf_c1, buf_c2, buf_cc, st_b, st_bc, p32, payc,
    picked, plhs, xat, khi, klo, shi, slo, acc_k, acc_s, buf_r, sc, buf_s,
    s_in, s_a1, r_a1, s_a2, r_a2, s_b1, r_b1, s_b2, r_b2, s_r, r_r, s_s, r_s,
):
    rem, div = lax.rem, lax.div
    buf_c = (buf_c0, buf_c1, buf_c2)
    blk = lax.axis_index("blk")
    half = lax.axis_index("pr")
    core = rem(blk, 2)
    zhi = rem(div(blk, 2), 4)
    x = rem(div(blk, 8), 4)
    y = div(blk, 32)
    m_a = y * 4 + zhi
    m_b = x * 2 + core
    a64 = half * 32 + m_a
    base_a = x * 8 + core
    base_b = y * 32 + zhi * 2

    def dev_a(k):
        m = rem(k, 32)
        return {"blk": div(m, 4) * 32 + rem(m, 4) * 2 + base_a, "pr": div(k, 32)}

    def dev_b(k):
        return {"blk": base_b + div(k, 2) * 8 + rem(k, 2), "pr": half}

    def send(src, dst, ssem, rsem, dev):
        pltpu.make_async_remote_copy(
            src_ref=src, dst_ref=dst, send_sem=ssem, recv_sem=rsem, device_id=dev, device_id_type=MESH
        ).start()

    fetches = [
        pltpu.make_async_copy(src, dst, s_in.at[n])
        for n, (src, dst) in enumerate(
            [(coords_h, coords), (alpha_h, alpha), (probes_h, probes), (solves_h, solves)]
        )
    ]
    for fetch in fetches:
        fetch.start()

    shifts = [plan[r, 0] for r in range(ROUNDS)]
    t_a = [(s // 32) * 4 + (s // 2) % 4 for s in shifts]
    t_b = [((s // 8) % 4) * 2 + s % 2 for s in shifts]

    barrier = pltpu.get_barrier_semaphore()

    def greet_a(k, _):
        pl.semaphore_signal(barrier, inc=1, device_id=dev_a(rem(a64 + k, 64)), device_id_type=MESH)
        return 0

    def greet_b(k, _):
        pl.semaphore_signal(barrier, inc=1, device_id=dev_b(rem(m_b + k, 8)), device_id_type=MESH)
        return 0

    lax.fori_loop(1, 64, greet_a, 0)
    lax.fori_loop(1, 8, greet_b, 0)

    fetches[0].wait()
    fetches[1].wait()
    for g in range(4):
        row = coords[g:g + 1, :] if g < 3 else alpha[...]
        for t in range(16):
            comps[g, t] = row[:, t * 128:(t + 1) * 128]
    fetches[2].wait()
    pl.semaphore_wait(barrier, 70)

    def probe_tile(hh, yy, zz):
        rows = pl.ds(pl.multiple_of(zz * 8, 8), 8)
        return rows, pl.ds(pl.multiple_of(hh * HALF + yy * 128, 128), 128)

    def spread_comps(k, _):
        m = rem(m_a + k, 32)
        send(comps.at[rem(m, 4), half * 8 + div(m, 4)], buf_ac.at[m_a], s_a1.at[0], r_a1.at[0], dev_a(half * 32 + m))
        return 0

    def spread_probes(k, _):
        d = rem(a64 + k, 64)
        m = rem(d, 32)
        rows, cols = probe_tile(div(d, 32), div(m, 4), rem(m, 4))
        send(probes.at[rows, cols], buf_a.at[a64], s_a1.at[1], r_a1.at[1], dev_a(d))
        return 0

    lax.fori_loop(1, 32, spread_comps, 0)
    lax.fori_loop(1, 64, spread_probes, 0)
    buf_ac[m_a] = comps[zhi, half * 8 + y]
    rows, cols = probe_tile(half, y, zhi)
    buf_a[a64] = probes[rows, cols]

    whole(buf_ac.at[0:31], r_a1.at[0])

    def select_ac(k, _):
        i = rem(m_a + k, 32)
        for r in range(ROUNDS):
            st_ac[i, r:r + 1, :] = buf_ac[i ^ t_a[r]]
        st_ac[i, 3:4, :] = jnp.zeros((1, 128), F32)
        send(st_ac.at[i], buf_bc.at[y, zhi], s_a2.at[3], r_a2.at[3], dev_a(half * 32 + i))
        return 0

    lax.fori_loop(1, 32, select_ac, 0)
    for r in range(ROUNDS):
        buf_bc[y, zhi, r:r + 1, :] = buf_ac[m_a ^ t_a[r]]
    buf_bc[y, zhi, 3:4, :] = jnp.zeros((1, 128), F32)

    whole(buf_a.at[0:63], r_a1.at[1])

    def select_a(r):
        def one(k, _):
            i = rem(m_a + k, 32)
            j = i ^ t_a[r]
            st_a[r, i, 0] = buf_a[j]
            st_a[r, i, 1] = buf_a[32 + j]
            send(st_a.at[r, i], buf_b.at[r, y, zhi], s_a2.at[r], r_a2.at[r], dev_a(half * 32 + i))
            return 0

        lax.fori_loop(1, 32, one, 0)
        j = m_a ^ t_a[r]
        buf_b[r, y, zhi, 0] = buf_a[j]
        buf_b[r, y, zhi, 1] = buf_a[32 + j]

    def spread_b(r):
        whole(st_a.at[r, 0:31], r_a2.at[r])

        def one(k, _):
            d = rem(m_b + k, 8)
            send(buf_b.at[r, d], buf_c[r].at[m_b], s_b1.at[r], r_b1.at[r], dev_b(d))
            return 0

        lax.fori_loop(1, 8, one, 0)
        buf_c[r][m_b] = buf_b[r, m_b]

    def select_b(r):
        whole(buf_c[r].at[0:7], r_b1.at[r])
        cols = pl.ds(pl.multiple_of(m_b * 128, 128), 128)

        def one(k, _):
            d = rem(m_b + k, 8)
            j = d ^ t_b[r]
            for hh in range(2):
                for g in range(4):
                    lo = (hh * 4 + g) * 8
                    st_b[r, d, lo:lo + 8, :] = buf_c[r][j, g, hh]
            send(st_b.at[r, d], p32.at[r, 0:64, cols], s_b2.at[r], r_b2.at[r], dev_b(d))
            return 0

        lax.fori_loop(1, 8, one, 0)
        j = m_b ^ t_b[r]
        for hh in range(2):
            for g in range(4):
                lo = (hh * 4 + g) * 8
                p32[r, lo:lo + 8, cols] = buf_c[r][j, g, hh]

    select_a(0)

    whole(st_ac.at[0:31], r_a2.at[3])

    def spread_bc(k, _):
        d = rem(m_b + k, 8)
        send(buf_bc.at[d], buf_cc.at[m_b], s_b1.at[3], r_b1.at[3], dev_b(d))
        return 0

    lax.fori_loop(1, 8, spread_bc, 0)
    buf_cc[m_b] = buf_bc[m_b]

    spread_b(0)
    select_a(1)

    whole(buf_cc.at[0:7], r_b1.at[3])

    def select_bc(k, _):
        d = rem(m_b + k, 8)
        for r in range(ROUNDS):
            for g in range(4):
                st_bc[d, g, r:r + 1, :] = buf_cc[d ^ t_b[r], g, r:r + 1, :]
        for g in range(4):
            st_bc[d, g, 3:4, :] = jnp.zeros((1, 128), F32)
        send(st_bc.at[d], payc.at[m_b], s_b2.at[3], r_b2.at[3], dev_b(d))
        return 0

    lax.fori_loop(1, 8, select_bc, 0)
    for r in range(ROUNDS):
        for g in range(4):
            payc[m_b, g, r:r + 1, :] = buf_cc[m_b ^ t_b[r], g, r:r + 1, :]

    select_b(0)
    select_a(2)

    fetches[3].wait()
    for j in range(64):
        picked[j:j + 1, :] = solves[pl.ds(pick[j], 1), :]
    acc_k[...] = jnp.zeros_like(acc_k)
    acc_s[...] = jnp.zeros_like(acc_s)
    noise = jnp.sum(
        picked[pl.ds(pl.multiple_of(half * 32, 32), 32), :] * probes[...], axis=0, keepdims=True
    )
    own = alpha[...]
    noise = 0.5 * own * own - noise * (1.0 / 64.0)

    def fold(row):
        total = row[:, 0:128]
        for t in range(1, 16):
            total = total + row[:, t * 128:(t + 1) * 128]
        return total

    sc[0, 0:1, :] = fold(noise)

    whole(st_bc.at[0:7], r_b2.at[3])
    for r in range(ROUNDS):
        for t in range(8):
            for g in range(4):
                p32[r, 64 + g:65 + g, t * 128:(t + 1) * 128] = payc[t, g, r:r + 1, :]
        p32[r, 68:72, :] = jnp.zeros((4, HALF), F32)

    spread_b(1)

    ka, kb, k2, k_slope = cst[0], cst[1], cst[2], cst[3]
    other = pl.ds(pl.multiple_of((1 - half) * 32, 32), 32)
    mine = pl.ds(pl.multiple_of(half * 32, 32), 32)
    mate = {"blk": blk, "pr": 1 - half}

    def step(t, _):
        r = div(t, STEPS)
        chunk = rem(t, STEPS)
        b = pl.multiple_of(chunk * TB, TB)

        @pl.when(chunk == 0)
        def _prepare():
            whole(st_b.at[r, 0:7], r_b2.at[r])
            p = jnp.concatenate([p32[r], jnp.zeros((8, HALF), F32)], 0)
            hi, lo = split(p)
            plhs[0:80, :] = hi
            plhs[80:160, :] = lo
            xat[...] = jnp.transpose(p32[r, 64:72, :])

        xb = [coords[c:c + 1, pl.ds(b, TB)] for c in range(3)]
        sum_k = sum_s = None
        for a in range(0, HALF, TA):
            for st in range(a, a + TA, STRIP):
                kern, slope = tile_terms(xat[st:st + STRIP, :], xb, ka, kb, k2)
                khi[st:st + STRIP, :], klo[st:st + STRIP, :] = split(kern)
                shi[st:st + STRIP, :], slo[st:st + STRIP, :] = split(slope)
            lhs = plhs[:, a:a + TA]

            def product(hi, lo):
                one = jnp.dot(lhs, hi[a:a + TA, :], preferred_element_type=F32)
                two = jnp.dot(lhs[:80], lo[a:a + TA, :], preferred_element_type=F32)
                return one[:72] + one[80:152] + two[:72]

            more_k, more_s = product(khi, klo), product(shi, slo)
            sum_k = more_k if sum_k is None else sum_k + more_k
            sum_s = more_s if sum_s is None else sum_s + more_s
        acc_k[:, pl.ds(b, TB)] += sum_k
        acc_s[:, pl.ds(b, TB)] += sum_s

        @pl.when(t == 0)
        def _hook_0():
            select_b(1)
            spread_b(2)

        @pl.when(t == 2)
        def _hook_2():
            select_b(2)

        @pl.when(r == ROUNDS - 1)
        def _share():
            send(acc_k.at[other, pl.ds(b, TB)], buf_r.at[0, :, pl.ds(b, TB)], s_r.at[0, chunk], r_r.at[0, chunk], mate)
            send(acc_s.at[other, pl.ds(b, TB)], buf_r.at[1, :, pl.ds(b, TB)], s_r.at[1, chunk], r_r.at[1, chunk], mate)

        return 0

    lax.fori_loop(0, ROUNDS * STEPS, step, 0)

    slope = acc_s[67:68, :] * own - jnp.sum(picked[...] * acc_s[0:64, :], axis=0, keepdims=True) * (1.0 / 64.0)
    sc[0, 1:2, :] = fold(slope) * k_slope
    m_z = zhi * 2 + half

    def dev_y(k):
        return {"blk": k * 32 + rem(blk, 32), "pr": half}

    def dev_z(k):
        return {"blk": y * 32 + div(k, 2) * 2 + base_a, "pr": rem(k, 2)}

    for n, (place, device) in enumerate([(y, dev_y), (m_z, dev_z), (m_b, dev_b)]):
        def scalars(k, _):
            send(sc.at[n], buf_s.at[n, place], s_s.at[n], r_s.at[n], device(rem(place + k, 8)))
            return 0

        lax.fori_loop(1, 8, scalars, 0)
        buf_s[n, place] = sc[n]
        whole(buf_s.at[n, 0:7], r_s.at[n])
        sc[n + 1] = jnp.sum(buf_s[n], axis=0)

    total = jnp.sum(sc[3], axis=1, keepdims=True) * (0.5 / COLS)
    grad_out[...] = jnp.broadcast_to(total, (2, 128))

    for c in range(STEPS):
        cols = slice(c * TB, (c + 1) * TB)
        whole(buf_r.at[0, :, cols], r_r.at[0, c])
        kz_out[:, cols] = acc_k[mine, cols] + buf_r[0, :, cols]
        whole(buf_r.at[1, :, cols], r_r.at[1, c])
        dkz_out[:, cols] = (acc_s[mine, cols] + buf_r[1, :, cols]) * k_slope

    whole(buf_ac.at[0:31], s_a1.at[0])
    whole(buf_a.at[0:63], s_a1.at[1])
    whole(st_ac.at[0:31], s_a2.at[3])
    whole(buf_cc.at[0:7], s_b1.at[3])
    whole(st_bc.at[0:7], s_b2.at[3])
    for r in range(ROUNDS):
        whole(st_a.at[r, 0:31], s_a2.at[r])
        whole(buf_c[r].at[0:7], s_b1.at[r])
        whole(st_b.at[r, 0:7], s_b2.at[r])
        whole(buf_s.at[r, 0:7], s_s.at[r])
    for c in range(STEPS):
        cols = slice(c * TB, (c + 1) * TB)
        whole(buf_r.at[0, :, cols], s_r.at[0, c])
        whole(buf_r.at[1, :, cols], s_r.at[1, c])


def local(coords, probes, solves, alpha, lengthscale, column_pick, plan):
    rate = math.sqrt(5.0) / lengthscale[0]
    cst = jnp.stack([
        rate * (-math.log2(math.e)), rate, rate * rate / 3.0, rate * rate / (3.0 * lengthscale[0])
    ])
    vm = pl.BlockSpec(memory_space=pltpu.VMEM)
    sm = pl.BlockSpec(memory_space=pltpu.SMEM)
    hb = pl.BlockSpec(memory_space=pl.ANY)
    V, dma = pltpu.VMEM, pltpu.SemaphoreType.DMA
    kz, dkz, grad = pl.pallas_call(
        body,
        out_shape=[
            jax.ShapeDtypeStruct((32, COLS), F32),
            jax.ShapeDtypeStruct((32, COLS), F32),
            jax.ShapeDtypeStruct((2, 128), F32),
        ],
        in_specs=[sm, sm, sm, hb, hb, hb, hb],
        out_specs=[vm, vm, vm],
        scratch_shapes=[
            V((3, COLS), F32), V((1, COLS), F32), V((32, COLS), F32), V((64, COLS), F32),
            V((4, 16, 1, 128), F32),
            V((64, 8, 128), F32), V((32, 1, 128), F32),
            V((ROUNDS, 32, 2, 8, 128), F32), V((32, 4, 128), F32),
            V((ROUNDS, 8, 4, 2, 8, 128), F32), V((8, 4, 4, 128), F32),
            V((8, 4, 2, 8, 128), F32), V((8, 4, 2, 8, 128), F32), V((8, 4, 2, 8, 128), F32),
            V((8, 4, 4, 128), F32),
            V((ROUNDS, 8, 64, 128), F32), V((8, 4, 4, 128), F32),
            V((ROUNDS, 72, HALF), F32), V((8, 4, 4, 128), F32),
            V((64, COLS), F32),
            V((160, HALF), BF16), V((HALF, 8), F32),
            V((HALF, TB), BF16), V((HALF, TB), BF16), V((HALF, TB), BF16), V((HALF, TB), BF16),
            V((72, COLS), F32), V((72, COLS), F32),
            V((2, 32, COLS), F32),
            V((4, 2, 128), F32), V((3, 8, 2, 128), F32),
            dma((4,)),
            dma((2,)), dma((2,)),
            dma((4,)), dma((4,)),
            dma((4,)), dma((4,)),
            dma((4,)), dma((4,)),
            dma((2, STEPS)), dma((2, STEPS)),
            dma((3,)), dma((3,)),
        ],
        compiler_params=pltpu.CompilerParams(
            collective_id=0, has_side_effects=True, vmem_limit_bytes=40 * 2 ** 20
        ),
    )(plan, column_pick, cst, coords, alpha.reshape(1, COLS), probes, solves)
    return kz, dkz, grad[:, 0]


def solution(mesh):
    placed = (P(None, "blk"), P("pr", "blk"), P(None, "blk"), P("blk"), P(), P(), P())
    return jax.shard_map(
        local,
        mesh=mesh,
        in_specs=placed,
        out_specs=(P("pr", "blk"), P("pr", "blk"), P()),
        check_vma=False,
    )
```

time: 118 us -> 106 us (0.90)
  Pallas kernels: 111 us -> 99.1 us
    pallas_call x1, Pallas kernels: 111 us -> 99.1 us  [local(): pl.pallas_call(body, out_shape=[jax.ShapeDtypeStruct((32, COLS), F32), ja...]
where the time goes in v2:
time: 106 us
  Pallas kernels  99.1 us (93%)
  local copies, waits for them, and re-layouts  5.44 us (5%)
  between operations  1.39 us (1%)
    pallas_call x1, Pallas kernels, local(): pl.pallas_call(body, out_shape=[jax.ShapeDtypeStruct((32, COLS), F32), ja...  99.1 us
    unnamed x14, local copies, waits for them, and re-layouts  4.81 us

profile of v2, /device:TPU:1, one launch (start us, length us, event | category | flops | bytes accessed | tf_op | source)
XLA Modules:
  0.0 106.0 jit_solution(2012273038345047760)
XLA Ops:
  1.3 0.0 copy-start.3
  1.4 0.0 copy-start.4
  1.4 0.1 pad_maximum_fusion.cst
  1.5 0.0 copy-start.5
  1.5 0.5 copy-done.3
  2.0 0.1 copy-done.4
  2.1 0.1 copy-done.5
  2.1 0.0 copy-start
  2.1 1.0 copy-done
  3.2 0.0 copy-start.1
  3.2 0.9 copy-done.1
  4.1 0.0 copy-start.2
  4.1 0.8 copy-done.2
  4.9 99.1 %shard_map.94 = (f32[32,2048]{1,0:T(8,128)S(1)}, f32[32,2048]{1,0:T(8,128)S(1)}, f32[2,128]{1,0:T(2,128)S(1)}) custom-call(s32[3,256]{1,0:T(4,128)S(1)} %copy-done.4, s32[64]{0:T(128)S(1)} %copy-done.5, f32[4]{0:T(128)S(1)} %pad_maximum_fusion.cst, f32[3,2048]{1,0:T(4,128)S(1)} %copy-done.2, f32[1,2048]{1,0:T(1,128)S(1)} %bitcast.1, ...), custom_call_target="tpu_custom_call" | custom-call | tf_op jit(solution)/shard_map/pallas_call | solution.py:369
  104.0 0.6 slice_reduce_fusion
  104.6 0.7 copy.13
  105.3 0.7 copy.14
Async XLA Ops:
  1.3 0.7 copy-start.3
  1.4 0.7 copy-start.4
  1.5 0.7 copy-start.5
  2.1 1.0 copy-start
  3.2 0.9 copy-start.1
  4.1 0.8 copy-start.2

commit v3 on v2

--- a/solution.py
+++ b/solution.py
@@ -11,8 +11,9 @@
 ROUNDS = 3
 COLS = 2048
 HALF = 1024
-TB = 512
-TA = 256
+TB = 256
+LAG = 11
+RING = 6
 STRIP = 16
 STEPS = COLS // TB
 
@@ -42,8 +43,8 @@
     kz_out, dkz_out, grad_out,
     coords, alpha, probes, solves,
     comps, buf_a, buf_ac, st_a, st_ac, buf_b, buf_bc, buf_c0, buf_c1, buf_c2, buf_cc, st_b, st_bc, p32, payc,
-    picked, plhs, xat, khi, klo, shi, slo, acc_k, acc_s, buf_r, sc, buf_s,
-    s_in, s_a1, r_a1, s_a2, r_a2, s_b1, r_b1, s_b2, r_b2, s_r, r_r, s_s, r_s,
+    picked, plhs, xat, even, odd, acc_k, acc_s, buf_r, sc, buf_s, buf_s2,
+    s_in, s_a1, r_a1, s_a2, r_a2, s_b1, r_b1, s_b2, r_b2, s_r, r_r, s_rs, r_rs, s_s, r_s,
 ):
     rem, div = lax.rem, lax.div
     buf_c = (buf_c0, buf_c1, buf_c2)
@@ -143,8 +144,6 @@
         buf_bc[y, zhi, r:r + 1, :] = buf_ac[m_a ^ t_a[r]]
     buf_bc[y, zhi, 3:4, :] = jnp.zeros((1, 128), F32)
 
-    whole(buf_a.at[0:63], r_a1.at[1])
-
     def select_a(r):
         def one(k, _):
             i = rem(m_a + k, 32)
@@ -191,8 +190,9 @@
                 lo = (hh * 4 + g) * 8
                 p32[r, lo:lo + 8, cols] = buf_c[r][j, g, hh]
 
-    select_a(0)
-
+    whole(buf_a.at[0:63], r_a1.at[1])
+    for r in range(ROUNDS):
+        select_a(r)
     whole(st_ac.at[0:31], r_a2.at[3])
 
     def spread_bc(k, _):
@@ -202,10 +202,6 @@
 
     lax.fori_loop(1, 8, spread_bc, 0)
     buf_cc[m_b] = buf_bc[m_b]
-
-    spread_b(0)
-    select_a(1)
-
     whole(buf_cc.at[0:7], r_b1.at[3])
 
     def select_bc(k, _):
@@ -223,123 +219,176 @@
         for g in range(4):
             payc[m_b, g, r:r + 1, :] = buf_cc[m_b ^ t_b[r], g, r:r + 1, :]
 
-    select_b(0)
-    select_a(2)
-
-    fetches[3].wait()
-    for j in range(64):
-        picked[j:j + 1, :] = solves[pl.ds(pick[j], 1), :]
-    acc_k[...] = jnp.zeros_like(acc_k)
-    acc_s[...] = jnp.zeros_like(acc_s)
-    noise = jnp.sum(
-        picked[pl.ds(pl.multiple_of(half * 32, 32), 32), :] * probes[...], axis=0, keepdims=True
-    )
-    own = alpha[...]
-    noise = 0.5 * own * own - noise * (1.0 / 64.0)
-
-    def fold(row):
-        total = row[:, 0:128]
-        for t in range(1, 16):
-            total = total + row[:, t * 128:(t + 1) * 128]
-        return total
-
-    sc[0, 0:1, :] = fold(noise)
-
     whole(st_bc.at[0:7], r_b2.at[3])
     for r in range(ROUNDS):
         for t in range(8):
             for g in range(4):
                 p32[r, 64 + g:65 + g, t * 128:(t + 1) * 128] = payc[t, g, r:r + 1, :]
         p32[r, 68:72, :] = jnp.zeros((4, HALF), F32)
-
-    spread_b(1)
+        xat[r] = jnp.transpose(p32[r, 64:72, :])
 
     ka, kb, k2, k_slope = cst[0], cst[1], cst[2], cst[3]
     other = pl.ds(pl.multiple_of((1 - half) * 32, 32), 32)
     mine = pl.ds(pl.multiple_of(half * 32, 32), 32)
     mate = {"blk": blk, "pr": 1 - half}
 
-    def step(t, _):
-        r = div(t, STEPS)
-        chunk = rem(t, STEPS)
-        b = pl.multiple_of(chunk * TB, TB)
-
-        @pl.when(chunk == 0)
-        def _prepare():
-            whole(st_b.at[r, 0:7], r_b2.at[r])
-            p = jnp.concatenate([p32[r], jnp.zeros((8, HALF), F32)], 0)
-            hi, lo = split(p)
-            plhs[0:80, :] = hi
-            plhs[80:160, :] = lo
-            xat[...] = jnp.transpose(p32[r, 64:72, :])
-
-        xb = [coords[c:c + 1, pl.ds(b, TB)] for c in range(3)]
-        sum_k = sum_s = None
-        for a in range(0, HALF, TA):
-            for st in range(a, a + TA, STRIP):
-                kern, slope = tile_terms(xat[st:st + STRIP, :], xb, ka, kb, k2)
-                khi[st:st + STRIP, :], klo[st:st + STRIP, :] = split(kern)
-                shi[st:st + STRIP, :], slo[st:st + STRIP, :] = split(slope)
-            lhs = plhs[:, a:a + TA]
-
-            def product(hi, lo):
-                one = jnp.dot(lhs, hi[a:a + TA, :], preferred_element_type=F32)
-                two = jnp.dot(lhs[:80], lo[a:a + TA, :], preferred_element_type=F32)
-                return one[:72] + one[80:152] + two[:72]
-
-            more_k, more_s = product(khi, klo), product(shi, slo)
-            sum_k = more_k if sum_k is None else sum_k + more_k
-            sum_s = more_s if sum_s is None else sum_s + more_s
-        acc_k[:, pl.ds(b, TB)] += sum_k
-        acc_s[:, pl.ds(b, TB)] += sum_s
-
-        @pl.when(t == 0)
+    def columns(t):
+        return pl.ds(pl.multiple_of(rem(t, STEPS) * TB, TB), TB)
+
+    def tiles(t, ring):
+        r, slot = div(t, STEPS), rem(div(t, 2), RING)
+        xb = [coords[c:c + 1, columns(t)] for c in range(3)]
+        for st in range(0, HALF, STRIP):
+            kern, slope = tile_terms(xat[r, st:st + STRIP, :], xb, ka, kb, k2)
+            ring[slot, 0, st:st + STRIP, :], ring[slot, 1, st:st + STRIP, :] = split(kern)
+            ring[slot, 2, st:st + STRIP, :], ring[slot, 3, st:st + STRIP, :] = split(slope)
+
+    def product(n, acc, t, ring):
+        r, slot = div(t, STEPS), rem(div(t, 2), RING)
+        one = jnp.dot(plhs[r], ring[slot, 2 * n], preferred_element_type=F32)
+        two = jnp.dot(plhs[r, 0:80, :], ring[slot, 2 * n + 1], preferred_element_type=F32)
+        acc[:, columns(t)] += one[:72] + one[80:152] + two[:72]
+
+    def products(t, ring):
+        product(0, acc_k, t, ring)
+        product(1, acc_s, t, ring)
+
+    def prepare(r):
+        whole(st_b.at[r, 0:7], r_b2.at[r])
+        hi, lo = split(jnp.concatenate([p32[r], jnp.zeros((8, HALF), F32)], 0))
+        plhs[r, 0:80, :] = hi
+        plhs[r, 80:160, :] = lo
+
+    def first(i, _):
+        tiles(2 * i, even)
+        tiles(2 * i + 1, odd)
+
+        @pl.when(i == 1)
+        def _hook_1():
+            spread_b(0)
+
+        @pl.when(i == 3)
+        def _hook_3():
+            select_b(0)
+
+        @pl.when(i == 4)
+        def _hook_4():
+            spread_b(1)
+
+        return 0
+
+    lax.fori_loop(0, LAG // 2, first, 0)
+    tiles(LAG - 1, even)
+
+    fetches[3].wait()
+    for j in range(64):
+        picked[j:j + 1, :] = solves[pl.ds(pick[j], 1), :]
+    acc_k[...] = jnp.zeros_like(acc_k)
+    acc_s[...] = jnp.zeros_like(acc_s)
+    noise = jnp.sum(picked[mine, :] * probes[...], axis=0, keepdims=True)
+    own = alpha[...]
+    noise = 0.5 * own * own - noise * (1.0 / 64.0)
+
+    def fold(row):
+        total = row[:, 0:128]
+        for t in range(1, 16):
+            total = total + row[:, t * 128:(t + 1) * 128]
+        return total
+
+    sc[0, 0:1, :] = fold(noise)
+    prepare(0)
+
+    def second(i, _):
+        tiles(2 * i + LAG, odd)
+        products(2 * i, even)
+        tiles(2 * i + LAG + 1, even)
+        products(2 * i + 1, odd)
+
+        @pl.when(i == 0)
         def _hook_0():
             select_b(1)
             spread_b(2)
 
-        @pl.when(t == 2)
+        @pl.when(i == 2)
         def _hook_2():
             select_b(2)
 
-        @pl.when(r == ROUNDS - 1)
-        def _share():
-            send(acc_k.at[other, pl.ds(b, TB)], buf_r.at[0, :, pl.ds(b, TB)], s_r.at[0, chunk], r_r.at[0, chunk], mate)
-            send(acc_s.at[other, pl.ds(b, TB)], buf_r.at[1, :, pl.ds(b, TB)], s_r.at[1, chunk], r_r.at[1, chunk], mate)
-
-        return 0
-
-    lax.fori_loop(0, ROUNDS * STEPS, step, 0)
+        @pl.when(i == 3)
+        def _hook_3():
+            prepare(1)
+
+        return 0
+
+    total_steps = ROUNDS * STEPS
+    pairs = (total_steps - LAG) // 2
+    lax.fori_loop(0, pairs, second, 0)
+    tiles(total_steps - 1, odd)
+    products(2 * pairs, even)
+    prepare(2)
+
+    def last_slope(i, _):
+        t = 2 * pairs + 1 + 2 * i
+        product(1, acc_s, t, odd)
+        product(1, acc_s, t + 1, even)
+        return 0
+
+    lax.fori_loop(0, LAG // 2, last_slope, 0)
+    product(1, acc_s, total_steps - 1, odd)
 
     slope = acc_s[67:68, :] * own - jnp.sum(picked[...] * acc_s[0:64, :], axis=0, keepdims=True) * (1.0 / 64.0)
     sc[0, 1:2, :] = fold(slope) * k_slope
-    m_z = zhi * 2 + half
-
-    def dev_y(k):
-        return {"blk": k * 32 + rem(blk, 32), "pr": half}
-
-    def dev_z(k):
-        return {"blk": y * 32 + div(k, 2) * 2 + base_a, "pr": rem(k, 2)}
-
-    for n, (place, device) in enumerate([(y, dev_y), (m_z, dev_z), (m_b, dev_b)]):
-        def scalars(k, _):
-            send(sc.at[n], buf_s.at[n, place], s_s.at[n], r_s.at[n], device(rem(place + k, 8)))
-            return 0
-
-        lax.fori_loop(1, 8, scalars, 0)
-        buf_s[n, place] = sc[n]
-        whole(buf_s.at[n, 0:7], r_s.at[n])
-        sc[n + 1] = jnp.sum(buf_s[n], axis=0)
-
-    total = jnp.sum(sc[3], axis=1, keepdims=True) * (0.5 / COLS)
-    grad_out[...] = jnp.broadcast_to(total, (2, 128))
-
+
+    def scalars_a(k, _):
+        send(sc.at[0], buf_s.at[a64], s_s.at[0], r_s.at[0], dev_a(rem(a64 + k, 64)))
+        return 0
+
+    lax.fori_loop(1, 64, scalars_a, 0)
+    buf_s[a64] = sc[0]
+
+    for c in range(2):
+        cols = slice(c * HALF, (c + 1) * HALF)
+        send(acc_s.at[other, cols], buf_r.at[1, :, cols], s_rs.at[c], r_rs.at[c], mate)
+
+    def share(t):
+        @pl.when(t >= total_steps - STEPS)
+        def _share():
+            chunk, cols = rem(t, STEPS), columns(t)
+            send(acc_k.at[other, cols], buf_r.at[0, :, cols], s_r.at[chunk], r_r.at[chunk], mate)
+
+    def last_kernel(i, _):
+        t = 2 * pairs + 1 + 2 * i
+        product(0, acc_k, t, odd)
+        share(t)
+        product(0, acc_k, t + 1, even)
+        share(t + 1)
+        return 0
+
+    lax.fori_loop(0, LAG // 2, last_kernel, 0)
+    product(0, acc_k, total_steps - 1, odd)
+    share(jnp.int32(total_steps - 1))
+
+    whole(buf_s.at[0:63], r_s.at[0])
+    sc[1] = jnp.sum(buf_s[...], axis=0)
+
+    def scalars_b(k, _):
+        send(sc.at[1], buf_s2.at[m_b], s_s.at[1], r_s.at[1], dev_b(rem(m_b + k, 8)))
+        return 0
+
+    lax.fori_loop(1, 8, scalars_b, 0)
+    buf_s2[m_b] = sc[1]
+
+    for c in range(2):
+        cols = slice(c * HALF, (c + 1) * HALF)
+        whole(buf_r.at[1, :, cols], r_rs.at[c])
+        dkz_out[:, cols] = (acc_s[mine, cols] + buf_r[1, :, cols]) * k_slope
     for c in range(STEPS):
         cols = slice(c * TB, (c + 1) * TB)
-        whole(buf_r.at[0, :, cols], r_r.at[0, c])
+        whole(buf_r.at[0, :, cols], r_r.at[c])
         kz_out[:, cols] = acc_k[mine, cols] + buf_r[0, :, cols]
-        whole(buf_r.at[1, :, cols], r_r.at[1, c])
-        dkz_out[:, cols] = (acc_s[mine, cols] + buf_r[1, :, cols]) * k_slope
+
+    whole(buf_s2.at[0:7], r_s.at[1])
+    total = jnp.sum(jnp.sum(buf_s2[...], axis=0), axis=1, keepdims=True) * (0.5 / COLS)
+    grad_out[...] = jnp.broadcast_to(total, (2, 128))
 
     whole(buf_ac.at[0:31], s_a1.at[0])
     whole(buf_a.at[0:63], s_a1.at[1])
@@ -350,11 +399,12 @@
         whole(st_a.at[r, 0:31], s_a2.at[r])
         whole(buf_c[r].at[0:7], s_b1.at[r])
         whole(st_b.at[r, 0:7], s_b2.at[r])
-        whole(buf_s.at[r, 0:7], s_s.at[r])
+    whole(buf_s.at[0:63], s_s.at[0])
+    whole(buf_s2.at[0:7], s_s.at[1])
+    for c in range(2):
+        whole(buf_r.at[1, :, c * HALF:(c + 1) * HALF], s_rs.at[c])
     for c in range(STEPS):
-        cols = slice(c * TB, (c + 1) * TB)
-        whole(buf_r.at[0, :, cols], s_r.at[0, c])
-        whole(buf_r.at[1, :, cols], s_r.at[1, c])
+        whole(buf_r.at[0, :, c * TB:(c + 1) * TB], s_r.at[c])
 
 
 def local(coords, probes, solves, alpha, lengthscale, column_pick, plan):
@@ -386,21 +436,22 @@
             V((ROUNDS, 8, 64, 128), F32), V((8, 4, 4, 128), F32),
             V((ROUNDS, 72, HALF), F32), V((8, 4, 4, 128), F32),
             V((64, COLS), F32),
-            V((160, HALF), BF16), V((HALF, 8), F32),
-            V((HALF, TB), BF16), V((HALF, TB), BF16), V((HALF, TB), BF16), V((HALF, TB), BF16),
+            V((ROUNDS, 160, HALF), BF16), V((ROUNDS, HALF, 8), F32),
+            V((RING, 4, HALF, TB), BF16), V((RING, 4, HALF, TB), BF16),
             V((72, COLS), F32), V((72, COLS), F32),
             V((2, 32, COLS), F32),
-            V((4, 2, 128), F32), V((3, 8, 2, 128), F32),
+            V((2, 2, 128), F32), V((64, 2, 128), F32), V((8, 2, 128), F32),
             dma((4,)),
             dma((2,)), dma((2,)),
             dma((4,)), dma((4,)),
             dma((4,)), dma((4,)),
             dma((4,)), dma((4,)),
-            dma((2, STEPS)), dma((2, STEPS)),
-            dma((3,)), dma((3,)),
+            dma((STEPS,)), dma((STEPS,)),
+            dma((2,)), dma((2,)),
+            dma((2,)), dma((2,)),
         ],
         compiler_params=pltpu.CompilerParams(
-            collective_id=0, has_side_effects=True, vmem_limit_bytes=40 * 2 ** 20
+            collective_id=0, has_side_effects=True, vmem_limit_bytes=63 * 2 ** 20
         ),
     )(plan, column_pick, cst, coords, alpha.reshape(1, COLS), probes, solves)
     return kz, dkz, grad[:, 0]

time: 106 us -> 101 us (0.953)
  Pallas kernels: 99.1 us -> 95.3 us
  local copies, waits for them, and re-layouts: 5.44 us -> 3.67 us
    pallas_call x1, Pallas kernels: 99.1 us -> 95.3 us  [local(): pl.pallas_call(body, out_shape=[jax.ShapeDtypeStruct((32, COLS), F32), ja...]
    unnamed x14 -> x6, local copies, waits for them, and re-layouts: 4.81 us -> 3.05 us
where the time goes in v3:
time: 101 us
  Pallas kernels  95.3 us (94%)
  local copies, waits for them, and re-layouts  3.67 us (4%)
  between operations  1.38 us (1%)
    pallas_call x1, Pallas kernels, local(): pl.pallas_call(body, out_shape=[jax.ShapeDtypeStruct((32, COLS), F32), ja...  95.3 us
    unnamed x6, local copies, waits for them, and re-layouts  3.05 us

profile of v3, /device:TPU:1, one launch (start us, length us, event | category | flops | bytes accessed | tf_op | source)
XLA Modules:
  0.0 101.0 jit_solution(5935252389968481023)
XLA Ops:
  1.4 0.6 pad_maximum_fusion.cst
  1.9 95.3 %shard_map.94 = (f32[32,2048]{1,0:T(8,128)}, f32[32,2048]{1,0:T(8,128)}, f32[2,128]{1,0:T(2,128)}) custom-call(s32[3,256]{1,0:T(4,128)} %plan.1, s32[64]{0:T(128)} %pick.1, f32[4]{0:T(128)} %pad_maximum_fusion.cst, f32[3,2048]{1,0:T(4,128)} %coords_h.1, f32[1,2048]{1,0:T(1,128)} %bitcast.1, f32[32,2048]{1,0:T(8,128)} %probes_h.1, f32[64,2048]{1,0:T(8,128)} %solves_h.1), custom_call_target="tpu_custom_call" | custom-call | tf_op jit(solution)/shard_map/pallas_call | solution.py:419
  97.3 0.0 copy-start.1
  97.3 0.6 copy-done.1
  97.9 0.6 slice_reduce_fusion
  98.6 0.0 copy-start
  98.6 1.7 %copy.13 = f32[32,2048]{1,0:T(8,128)} copy(f32[32,2048]{1,0:T(8,128)} %get-tuple-element.12) | data formatting | bytes 524288
  100.3 0.0 copy-done
  100.3 0.7 copy.14
Async XLA Ops:
  97.3 0.6 copy-start.1
  98.6 1.7 %copy-start = (f32[32,2048]{1,0:T(8,128)S(1)}, f32[32,2048]{1,0:T(8,128)}, u32[]{:S(2)}) copy-start(f32[32,2048]{1,0:T(8,128)} %get-tuple-element.13) | copy-start | bytes 786436

commit v4 on v3

--- a/solution.py
+++ b/solution.py
@@ -12,8 +12,8 @@
 COLS = 2048
 HALF = 1024
 TB = 256
-LAG = 11
-RING = 6
+LAG = 15
+RING = 8
 STRIP = 16
 STEPS = COLS // TB
 
@@ -129,6 +129,26 @@
     rows, cols = probe_tile(half, y, zhi)
     buf_a[a64] = probes[rows, cols]
 
+    other = pl.ds(pl.multiple_of((1 - half) * 32, 32), 32)
+    mine = pl.ds(pl.multiple_of(half * 32, 32), 32)
+    mate = {"blk": blk, "pr": 1 - half}
+
+    fetches[3].wait()
+    for j in range(64):
+        picked[j:j + 1, :] = solves[pl.ds(pick[j], 1), :]
+    acc_k[...] = jnp.zeros_like(acc_k)
+    acc_s[...] = jnp.zeros_like(acc_s)
+    noise = jnp.sum(picked[mine, :] * probes[...], axis=0, keepdims=True)
+    own = alpha[...]
+    noise = 0.5 * own * own - noise * (1.0 / 64.0)
+
+    def fold(row):
+        total = row[:, 0:128]
+        for t in range(1, 16):
+            total = total + row[:, t * 128:(t + 1) * 128]
+        return total
+
+    sc[0, 0:1, :] = fold(noise)
     whole(buf_ac.at[0:31], r_a1.at[0])
 
     def select_ac(k, _):
@@ -228,9 +248,6 @@
         xat[r] = jnp.transpose(p32[r, 64:72, :])
 
     ka, kb, k2, k_slope = cst[0], cst[1], cst[2], cst[3]
-    other = pl.ds(pl.multiple_of((1 - half) * 32, 32), 32)
-    mine = pl.ds(pl.multiple_of(half * 32, 32), 32)
-    mate = {"blk": blk, "pr": 1 - half}
 
     def columns(t):
         return pl.ds(pl.multiple_of(rem(t, STEPS) * TB, TB), TB)
@@ -263,39 +280,29 @@
         tiles(2 * i, even)
         tiles(2 * i + 1, odd)
 
-        @pl.when(i == 1)
-        def _hook_1():
+        @pl.when(i == 0)
+        def _hook_0():
             spread_b(0)
 
-        @pl.when(i == 3)
-        def _hook_3():
+        @pl.when(i == 2)
+        def _hook_2():
+            spread_b(1)
             select_b(0)
 
         @pl.when(i == 4)
         def _hook_4():
-            spread_b(1)
+            spread_b(2)
+            select_b(1)
+
+        @pl.when(i == 6)
+        def _hook_6():
+            select_b(2)
 
         return 0
 
     lax.fori_loop(0, LAG // 2, first, 0)
     tiles(LAG - 1, even)
 
-    fetches[3].wait()
-    for j in range(64):
-        picked[j:j + 1, :] = solves[pl.ds(pick[j], 1), :]
-    acc_k[...] = jnp.zeros_like(acc_k)
-    acc_s[...] = jnp.zeros_like(acc_s)
-    noise = jnp.sum(picked[mine, :] * probes[...], axis=0, keepdims=True)
-    own = alpha[...]
-    noise = 0.5 * own * own - noise * (1.0 / 64.0)
-
-    def fold(row):
-        total = row[:, 0:128]
-        for t in range(1, 16):
-            total = total + row[:, t * 128:(t + 1) * 128]
-        return total
-
-    sc[0, 0:1, :] = fold(noise)
     prepare(0)
 
     def second(i, _):
@@ -304,24 +311,12 @@
         tiles(2 * i + LAG + 1, even)
         products(2 * i + 1, odd)
 
-        @pl.when(i == 0)
-        def _hook_0():
-            select_b(1)
-            spread_b(2)
-
-        @pl.when(i == 2)
-        def _hook_2():
-            select_b(2)
-
-        @pl.when(i == 3)
-        def _hook_3():
-            prepare(1)
-
         return 0
 
     total_steps = ROUNDS * STEPS
     pairs = (total_steps - LAG) // 2
     lax.fori_loop(0, pairs, second, 0)
+    prepare(1)
     tiles(total_steps - 1, odd)
     products(2 * pairs, even)
     prepare(2)
@@ -388,7 +383,8 @@
 
     whole(buf_s2.at[0:7], r_s.at[1])
     total = jnp.sum(jnp.sum(buf_s2[...], axis=0), axis=1, keepdims=True) * (0.5 / COLS)
-    grad_out[...] = jnp.broadcast_to(total, (2, 128))
+    grad_out[0] = total[0, 0]
+    grad_out[1] = total[1, 0]
 
     whole(buf_ac.at[0:31], s_a1.at[0])
     whole(buf_a.at[0:63], s_a1.at[1])
@@ -421,10 +417,10 @@
         out_shape=[
             jax.ShapeDtypeStruct((32, COLS), F32),
             jax.ShapeDtypeStruct((32, COLS), F32),
-            jax.ShapeDtypeStruct((2, 128), F32),
+            jax.ShapeDtypeStruct((2,), F32),
         ],
         in_specs=[sm, sm, sm, hb, hb, hb, hb],
-        out_specs=[vm, vm, vm],
+        out_specs=[vm, vm, sm],
         scratch_shapes=[
             V((3, COLS), F32), V((1, COLS), F32), V((32, COLS), F32), V((64, COLS), F32),
             V((4, 16, 1, 128), F32),
@@ -454,7 +450,7 @@
             collective_id=0, has_side_effects=True, vmem_limit_bytes=63 * 2 ** 20
         ),
     )(plan, column_pick, cst, coords, alpha.reshape(1, COLS), probes, solves)
-    return kz, dkz, grad[:, 0]
+    return kz, dkz, grad
 
 
 def solution(mesh):

time: 101 us -> 97.1 us (0.961)
  Pallas kernels: 95.3 us -> 92 us
    pallas_call x1, Pallas kernels: 95.3 us -> 92 us  [local(): pl.pallas_call(body, out_shape=[jax.ShapeDtypeStruct((32, COLS), F32), ja...]
    unnamed x6 -> x7, local copies, waits for them, and re-layouts: 3.05 us -> 2.93 us
where the time goes in v4:
time: 97.1 us; the launch traced here: 96.9 us
  Pallas kernels  92 us (95%)
  local copies, waits for them, and re-layouts  2.93 us (3%)
  between operations  1.38 us (1%)
    pallas_call x1, Pallas kernels, local(): pl.pallas_call(body, out_shape=[jax.ShapeDtypeStruct((32, COLS), F32), ja...  92 us
    unnamed x7, local copies, waits for them, and re-layouts  2.93 us

profile of v4, /device:TPU:1, one launch (start us, length us, event | category | flops | bytes accessed | tf_op | source)
XLA Modules:
  0.0 96.9 jit_solution(5190000712545681895)
XLA Ops:
  1.4 0.6 pad_maximum_fusion.cst
  1.9 92.0 %shard_map.94 = (f32[32,2048]{1,0:T(8,128)}, f32[32,2048]{1,0:T(8,128)}, f32[2]{0:T(128)}) custom-call(s32[3,256]{1,0:T(4,128)} %plan.1, s32[64]{0:T(128)} %pick.1, f32[4]{0:T(128)} %pad_maximum_fusion.cst, f32[3,2048]{1,0:T(4,128)} %coords_h.1, f32[1,2048]{1,0:T(1,128)} %bitcast.1, f32[32,2048]{1,0:T(8,128)} %probes_h.1, f32[64,2048]{1,0:T(8,128)} %solves_h.1), custom_call_target="tpu_custom_call" | custom-call | tf_op jit(solution)/shard_map/pallas_call | solution.py:415
  94.0 0.0 copy-start
  94.0 1.7 %copy.14 = f32[32,2048]{1,0:T(8,128)} copy(f32[32,2048]{1,0:T(8,128)} %get-tuple-element.6) | data formatting | bytes 524288
  95.7 0.0 copy-done
  95.7 0.0 copy-start.1
  95.7 0.7 copy.15
  96.4 0.0 copy-done.1
  96.4 0.5 copy.16
Async XLA Ops:
  94.0 1.7 %copy-start = (f32[32,2048]{1,0:T(8,128)S(1)}, f32[32,2048]{1,0:T(8,128)}, u32[]{:S(2)}) copy-start(f32[32,2048]{1,0:T(8,128)} %get-tuple-element.7) | copy-start | bytes 786436
  95.7 0.7 copy-start.1

commit v5 on v4

--- a/solution.py
+++ b/solution.py
@@ -23,15 +23,15 @@
     return hi, (value - hi.astype(F32)).astype(BF16)
 
 
-def tile_terms(xa, xb, ka, kb, k2):
+def tile_terms(xa, xb, ka, k1, k0):
     d2 = None
     for comp in range(3):
         off = xa[:, comp:comp + 1] - xb[comp]
         d2 = off * off if d2 is None else d2 + off * off
     dist = d2 * lax.rsqrt(jnp.maximum(d2, 1e-30))
     decay = jnp.exp2(dist * ka)
-    bell = (1.0 + dist * kb) * decay
-    return bell + (d2 * k2) * decay, d2 * bell
+    bell = (k0 + dist * k1) * decay
+    return bell + d2 * decay, d2 * bell
 
 
 def whole(ref, sem):
@@ -247,7 +247,7 @@
         p32[r, 68:72, :] = jnp.zeros((4, HALF), F32)
         xat[r] = jnp.transpose(p32[r, 64:72, :])
 
-    ka, kb, k2, k_slope = cst[0], cst[1], cst[2], cst[3]
+    ka, k1, k0, k_kernel, k_slope = cst[0], cst[1], cst[2], cst[3], cst[4]
 
     def columns(t):
         return pl.ds(pl.multiple_of(rem(t, STEPS) * TB, TB), TB)
@@ -256,7 +256,7 @@
         r, slot = div(t, STEPS), rem(div(t, 2), RING)
         xb = [coords[c:c + 1, columns(t)] for c in range(3)]
         for st in range(0, HALF, STRIP):
-            kern, slope = tile_terms(xat[r, st:st + STRIP, :], xb, ka, kb, k2)
+            kern, slope = tile_terms(xat[r, st:st + STRIP, :], xb, ka, k1, k0)
             ring[slot, 0, st:st + STRIP, :], ring[slot, 1, st:st + STRIP, :] = split(kern)
             ring[slot, 2, st:st + STRIP, :], ring[slot, 3, st:st + STRIP, :] = split(slope)
 
@@ -310,25 +310,32 @@
         products(2 * i, even)
         tiles(2 * i + LAG + 1, even)
         products(2 * i + 1, odd)
-
         return 0
 
     total_steps = ROUNDS * STEPS
     pairs = (total_steps - LAG) // 2
-    lax.fori_loop(0, pairs, second, 0)
+    lax.fori_loop(0, 2, second, 0)
     prepare(1)
+
+    def third(i, _):
+        tiles(2 * i + LAG, odd)
+        products(2 * i, even)
+        product(1, acc_s, 2 * i + 4, even)
+        tiles(2 * i + LAG + 1, even)
+        products(2 * i + 1, odd)
+        product(1, acc_s, 2 * i + 5, odd)
+        return 0
+
+    lax.fori_loop(2, pairs, third, 0)
     tiles(total_steps - 1, odd)
-    products(2 * pairs, even)
     prepare(2)
 
     def last_slope(i, _):
-        t = 2 * pairs + 1 + 2 * i
-        product(1, acc_s, t, odd)
-        product(1, acc_s, t + 1, even)
-        return 0
-
-    lax.fori_loop(0, LAG // 2, last_slope, 0)
-    product(1, acc_s, total_steps - 1, odd)
+        product(1, acc_s, 2 * i, even)
+        product(1, acc_s, 2 * i + 1, odd)
+        return 0
+
+    lax.fori_loop(pairs + 2, total_steps // 2, last_slope, 0)
 
     slope = acc_s[67:68, :] * own - jnp.sum(picked[...] * acc_s[0:64, :], axis=0, keepdims=True) * (1.0 / 64.0)
     sc[0, 1:2, :] = fold(slope) * k_slope
@@ -351,16 +358,13 @@
             send(acc_k.at[other, cols], buf_r.at[0, :, cols], s_r.at[chunk], r_r.at[chunk], mate)
 
     def last_kernel(i, _):
-        t = 2 * pairs + 1 + 2 * i
-        product(0, acc_k, t, odd)
-        share(t)
-        product(0, acc_k, t + 1, even)
-        share(t + 1)
-        return 0
-
-    lax.fori_loop(0, LAG // 2, last_kernel, 0)
-    product(0, acc_k, total_steps - 1, odd)
-    share(jnp.int32(total_steps - 1))
+        product(0, acc_k, 2 * i, even)
+        share(2 * i)
+        product(0, acc_k, 2 * i + 1, odd)
+        share(2 * i + 1)
+        return 0
+
+    lax.fori_loop(pairs, total_steps // 2, last_kernel, 0)
 
     whole(buf_s.at[0:63], r_s.at[0])
     sc[1] = jnp.sum(buf_s[...], axis=0)
@@ -379,7 +383,7 @@
     for c in range(STEPS):
         cols = slice(c * TB, (c + 1) * TB)
         whole(buf_r.at[0, :, cols], r_r.at[c])
-        kz_out[:, cols] = acc_k[mine, cols] + buf_r[0, :, cols]
+        kz_out[:, cols] = (acc_k[mine, cols] + buf_r[0, :, cols]) * k_kernel
 
     whole(buf_s2.at[0:7], r_s.at[1])
     total = jnp.sum(jnp.sum(buf_s2[...], axis=0), axis=1, keepdims=True) * (0.5 / COLS)
@@ -405,8 +409,10 @@
 
 def local(coords, probes, solves, alpha, lengthscale, column_pick, plan):
     rate = math.sqrt(5.0) / lengthscale[0]
+    square = rate * rate / 3.0
     cst = jnp.stack([
-        rate * (-math.log2(math.e)), rate, rate * rate / 3.0, rate * rate / (3.0 * lengthscale[0])
+        rate * (-math.log2(math.e)), rate / square, 1.0 / square, square,
+        square * (square / lengthscale[0]),
     ])
     vm = pl.BlockSpec(memory_space=pltpu.VMEM)
     sm = pl.BlockSpec(memory_space=pltpu.SMEM)

time: 97.1 us -> 96.3 us (level)
    pallas_call x1, Pallas kernels: 92 us -> 91.1 us  [local(): pl.pallas_call(body, out_shape=[jax.ShapeDtypeStruct((32, COLS), F32), ja...]
where the time goes in v5:
time: 96.3 us; the launch traced here: 96.1 us
  Pallas kernels  91.1 us (95%)
  local copies, waits for them, and re-layouts  3.57 us (4%)
  between operations  1.46 us (2%)
    pallas_call x1, Pallas kernels, local(): pl.pallas_call(body, out_shape=[jax.ShapeDtypeStruct((32, COLS), F32), ja...  91.1 us
    unnamed x7, local copies, waits for them, and re-layouts  2.93 us

profile of v5, /device:TPU:1, one launch (start us, length us, event | category | flops | bytes accessed | tf_op | source)
XLA Modules:
  0.0 96.1 jit_solution(5060051661975689099)
XLA Ops:
  1.4 0.6 stack.23.cst
  2.1 91.1 %shard_map.94 = (f32[32,2048]{1,0:T(8,128)}, f32[32,2048]{1,0:T(8,128)}, f32[2]{0:T(128)}) custom-call(s32[3,256]{1,0:T(4,128)} %plan.1, s32[64]{0:T(128)} %pick.1, f32[5]{0:T(128)} %stack.23.cst, f32[3,2048]{1,0:T(4,128)} %coords_h.1, f32[1,2048]{1,0:T(1,128)} %bitcast.10, f32[32,2048]{1,0:T(8,128)} %probes_h.1, f32[64,2048]{1,0:T(8,128)} %solves_h.1), custom_call_target="tpu_custom_call" | custom-call | tf_op jit(solution)/shard_map/pallas_call | solution.py:421
  93.1 0.0 copy-start
  93.1 1.7 %copy.14 = f32[32,2048]{1,0:T(8,128)} copy(f32[32,2048]{1,0:T(8,128)} %get-tuple-element.6) | data formatting | bytes 524288
  94.9 0.0 copy-done
  94.9 0.0 copy-start.1
  94.9 0.7 copy.15
  95.6 0.0 copy-done.1
  95.6 0.5 copy.16
Async XLA Ops:
  93.1 1.7 %copy-start = (f32[32,2048]{1,0:T(8,128)S(1)}, f32[32,2048]{1,0:T(8,128)}, u32[]{:S(2)}) copy-start(f32[32,2048]{1,0:T(8,128)} %get-tuple-element.7) | copy-start | bytes 786436
  94.9 0.7 copy-start.1
